TPU v7x, 128 devices: a whole 4x4x4 slice. The times are simulated.
128 devices in a mesh: replica: 8 (over x, core), tensor: 16 (over z, y).
Axes of the slice: x: 4, y: 4, z: 4, core: 2. Of those that a mesh axis runs over, the one named last changes fastest.
Arguments:
- gated_hidden: bfloat16 [2, 1024, 14336], P(None, 'replica', 'tensor'), may hold values from -6 to 6
- coded_weight: bfloat16 [14336, 8192], P('tensor'), may hold values from -6 to 6, as said below
- block_exponent: int32 [448, 8192], P('tensor'), may hold values from 117 to 120
- stream_input: bfloat16 [2, 1024, 8192], P(None, 'replica', 'tensor'), may hold values from -6 to 6
- lower_layer: bfloat16 [1024, 8192], P('replica', 'tensor'), may hold values from -6 to 6
- middle_layer: bfloat16 [1024, 8192], P('replica', 'tensor'), may hold values from -6 to 6
- prior_lower: bfloat16 [1024, 8192], P('replica', 'tensor'), may hold values from -6 to 6
- prior_middle: bfloat16 [1024, 8192], P('replica', 'tensor'), may hold values from -6 to 6
- prior_upper: bfloat16 [1024, 8192], P('replica', 'tensor'), may hold values from -6 to 6
- accepted: int32 [1024], P('replica'), may hold values from 0 to 2, as said below
- draft_input_weight: float32 [3, 8192, 8192], P(None, 'tensor', 'replica'), may hold values from -0.44194174 to 0.44194174
- draft_gain: float32 [8192], P('replica'), may hold values from 0.5 to 2
Outputs:
- upper_layer: bfloat16 [2, 1024, 8192], P(None, 'replica', 'tensor')
- new_weight: bfloat16 [3, 8192, 8192], P(None, 'tensor', 'replica')
Inputs may be any that keep to these rules, and one draw needn't show every extreme that they name: `coded_weight`: the values of the FP4 E2M1 grid: 0, 0.5, 1, 1.5, 2, 3, 4, 6 and their negatives. The accepted lengths of the 128 rows of one replica (aligned blocks of 128 rows) sum to at most 192, and to exactly that in at least one block.
All inputs are finite; a program needn't handle non-finite values.
Results may differ from a plain program's by a relative error of at most 0.005.
Values may be sent and summed in bfloat16 or wider, within the bound.
No kernel may reach another device: no remote copies, remote signals or barrier semaphores. Data moves between devices by JAX's collectives and lax.ppermute only.
A program may use at most 128 MiB of HBM per device.

v0:
```python
import jax
import jax.numpy as jnp
from jax import lax
from jax.sharding import PartitionSpec as P

step_rate = 8.0
epsilon = 1e-06


def spread(array, axis, root):
    mine = lax.axis_index(axis) == root
    return lax.psum(jnp.where(mine, array, jnp.zeros_like(array)), axis)


def body(
    gated_hidden,
    coded_weight,
    block_exponent,
    stream_input,
    lower_layer,
    middle_layer,
    prior_lower,
    prior_middle,
    prior_upper,
    accepted,
    draft_input_weight,
    draft_gain,
):
    steps, rows, unit_count = gated_hidden.shape
    width = coded_weight.shape[1]
    feature_slice = stream_input.shape[2]
    block_count = block_exponent.shape[0]
    tokens = gated_hidden.reshape(steps * rows, unit_count)
    factor = jnp.exp2(block_exponent.astype(jnp.float32) - 127.0).astype(jnp.bfloat16)
    columns = (
        coded_weight.reshape(
            block_count, unit_count // block_count, feature_slice * lax.axis_size("tensor")
        )
        * factor[:, None, :]
    ).reshape(unit_count, feature_slice * lax.axis_size("tensor"))
    summed = lax.psum_scatter(
        lax.dot_general(
            columns, tokens, (((0,), (1,)), ((), ())), preferred_element_type=jnp.float32
        ),
        "tensor",
        scatter_dimension=0,
        tiled=True,
    )
    upper_layer = (
        stream_input.astype(jnp.float32) + summed.T.reshape(steps, rows, feature_slice)
    ).astype(jnp.bfloat16)
    first = jnp.concatenate([prior_lower, prior_middle, prior_upper], axis=1)
    second = jnp.concatenate([lower_layer, middle_layer, upper_layer[0]], axis=1)
    payload = jnp.concatenate(
        [
            jnp.concatenate([first, second], axis=0),
            upper_layer.reshape(steps * rows, feature_slice),
        ],
        axis=1,
    )
    replicas = lax.axis_size("replica")
    tensors = lax.axis_size("tensor")
    gathered, lengths = (
        lax.all_gather(payload, "replica", axis=0, tiled=True),
        lax.all_gather(accepted, "replica", axis=0, tiled=True),
    )
    live = (
        jnp.arange(steps, dtype=jnp.int32)[None, :, None] < lengths.reshape(replicas, 1, rows)
    ).reshape(-1)
    current_weight = live.astype(jnp.float32)
    total = gathered.shape[0]
    input_rows = (
        gathered[:, : 3 * feature_slice].reshape(total, 3, feature_slice).astype(jnp.float32)
    )
    target_slice = gathered[:, 3 * feature_slice :]
    group = tensors // replicas
    leader = lax.axis_index("replica") * group
    received = []
    for offset in range(group):
        received.append(spread(target_slice, "tensor", leader + offset))
    targets = jnp.concatenate(received, axis=1)
    slots_all = steps * rows * replicas
    partial_result = jnp.einsum(
        "wmg,mgf->wf", input_rows, draft_input_weight, precision=lax.Precision.HIGHEST
    )
    drafted = lax.psum(partial_result, "tensor")
    squares = lax.psum(jnp.sum(drafted * drafted, axis=1), "replica")
    scale = lax.rsqrt(squares / width + epsilon)
    output = draft_gain * drafted * scale[:, None]
    error = draft_gain * (
        current_weight[:, None] * (output - targets.astype(jnp.float32)) / slots_all
    )
    inner = lax.psum(jnp.sum(error * drafted, axis=1), "replica")
    loss_gradient = scale[:, None] * error - drafted * (scale**3 * inner / width)[:, None]
    update_step = jnp.einsum(
        "zag,zh->agh", input_rows, loss_gradient, precision=lax.Precision.HIGHEST
    )
    new_weight = (draft_input_weight - step_rate * update_step).astype(jnp.bfloat16)
    return (upper_layer, new_weight)


def solution(mesh):
    return jax.shard_map(
        body,
        mesh=mesh,
        in_specs=(
            P(None, "replica", "tensor"),
            P("tensor", None),
            P("tensor", None),
            P(None, "replica", "tensor"),
            P("replica", "tensor"),
            P("replica", "tensor"),
            P("replica", "tensor"),
            P("replica", "tensor"),
            P("replica", "tensor"),
            P("replica"),
            P(None, "tensor", "replica"),
            P("replica"),
        ),
        out_specs=(P(None, "replica", "tensor"), P(None, "tensor", "replica")),
        check_vma=False,
    )
```

profile of v0, /device:TPU:0, one launch (start us, length us, event | category | flops | bytes accessed | tf_op | source)
XLA Modules:
  0.0 509.0 jit_solution(4017757699604506643)
XLA Ops:
  7.2 0.0 copy-start
  7.2 0.0 reduce-scatter.2.cloned.1.call-start
  7.2 1.5 exponential_convert_fusion
  8.7 7.6 %bitcast_multiply_fusion = bf16[896,8192]{1,0:T(8,128)(2,1)S(1)} fusion(bf16[896,8192]{1,0:T(8,128)(2,1)} %param.13, bf16[28,8192]{1,0:T(8,128)(2,1)S(1)} %exponential_convert_fusion), kind=kLoop, calls=%fused_computation | loop fusion | flops 7340032 | bytes 29818880 | tf_op jit(solution)/shard_map/mul | solution.py:36
  16.3 7.1 %fusion.15 = f32[8192,256]{1,0:T(8,128)} fusion(bf16[896,8192]{1,0:T(8,128)(2,1)S(1)} %bitcast_multiply_fusion, bf16[256,896]{1,0:T(8,128)(2,1)S(1)} %bitcast.24), kind=kOutput, calls=%fused_computation.30 | convolution fusion | flops 3758096384 | bytes 23527424 | tf_op jit(solution)/shard_map/dot_general | solution.py:42
  23.4 0.0 copy-start.8
  23.4 0.0 reduce-scatter.2.cloned.1.call-update
  23.4 0.0 all-gather.3.cloned.1.call-start
  23.5 87.8 %reduce-scatter.2.cloned.1.call-done = f32[512,256]{1,0:T(8,128)} async-done(((f32[8192,256]{1,0:T(8,128)}), f32[512,256]{1,0:T(8,128)}) %reduce-scatter.2.cloned.1.call-update) | async-done | bytes 524304 | tf_op jit(solution)/shard_map/reduce_scatter | solution.py:41
  111.3 1.2 copy.23
  112.6 0.1 add_convert_fusion
  112.6 0.0 copy-start.3
  112.7 1.1 pad_maximum_fusion.2
  113.8 0.0 all-gather.3.cloned.1.call-update
  113.9 0.2 all-reduce.4.cloned.1.call-start
  114.1 48.8 %all-gather.3.cloned.1.call-done = bf16[2048,2048]{1,0:T(8,128)(2,1)} async-done(((bf16[256,2048]{1,0:T(8,128)(2,1)}), bf16[2048,2048]{1,0:T(8,128)(2,1)}) %all-gather.3.cloned.1.call-update) | async-done | bytes 8388624 | tf_op jit(solution)/shard_map/all_gather | solution.py:64
  162.9 5.8 %slice.13 = bf16[2048,1536]{1,0:T(8,128)(2,1)} slice(bf16[2048,2048]{1,0:T(8,128)(2,1)} %all-gather.3.cloned.1.call-done), slice={[0:2048], [0:1536]} | slice | bytes 12582912 | tf_op jit(solution)/shard_map/slice | solution.py:73
  168.7 8.6 %copy.20 = bf16[2048,1536]{0,1:T(8,128)(2,1)} copy(bf16[2048,1536]{1,0:T(8,128)(2,1)} %slice.13) | data formatting | bytes 12582912 | tf_op jit(solution)/shard_map/slice | solution.py:73
  177.4 26.1 %convolution_bitcast_fusion = f32[2048,1024]{1,0:T(8,128)} fusion(bf16[2048,3,512]{0,2,1:T(8,128)(2,1)} %bitcast.25, f32[3,512,1024]{2,1,0:T(8,128)} %param.22), kind=kOutput, calls=%fused_computation.10 | convolution fusion | flops 38654705664 | bytes 20971520 | tf_op jit(solution)/shard_map/wmg,mgf->wf/dot_general | solution.py:83
  203.4 0.0 all-reduce.4.cloned.1.call-update
  203.4 0.0 all-reduce.6.cloned.1.call-start
  203.5 3.9 broadcast_select_fusion.1
  207.4 0.0 all-reduce.6.cloned.1.call-update
  207.4 8.8 %all-gather = s32[8,1,128]{2,1,0:T(1,128)S(1)} all-gather(s32[1,1,128]{2,1,0:T(1,128)S(1)} %bitcast.33), channel_id=1, replica_groups=mesh['replica'=8,'tensor'=16] {'replica'}, dimensions={0}, use_global_device_ids=true | all-gather | bytes 4608 | tf_op jit(solution)/shard_map/all_gather | solution.py:65
  216.2 129.5 %all-reduce.4.cloned.1.call-done = f32[2048,1024]{1,0:T(8,128)} async-done(((f32[2048,1024]{1,0:T(8,128)}), f32[2048,1024]{1,0:T(8,128)}) %all-reduce.4.cloned.1.call-update) | async-done | bytes 8388624 | tf_op jit(solution)/shard_map/psum | solution.py:86
  345.7 4.0 multiply_reduce_fusion.1
  349.7 14.7 %psum.36 = f32[2048]{0:T(1024)S(1)} all-reduce(f32[2048]{0:T(1024)S(1)} %multiply_reduce_fusion.1), channel_id=1, replica_groups=mesh['replica'=8,'tensor'=16] {'replica'}, use_global_device_ids=true, to_apply=%region_3.4 | all-reduce | flops 2048 | bytes 16384 | tf_op jit(solution)/shard_map/psum | solution.py:87
  364.4 88.2 %all-reduce.6.cloned.1.call-done = (bf16[2048,512]{1,0:T(8,128)(2,1)}, bf16[2048,512]{1,0:T(8,128)(2,1)}) async-done(((bf16[2048,512]{1,0:T(8,128)(2,1)}, bf16[2048,512]{1,0:T(8,128)(2,1)}), (bf16[2048,512]{1,0:T(8,128)(2,1)}, bf16[2048,512]{1,0:T(8,128)(2,1)})) %all-reduce.6.cloned.1.call-update) | async-done | bytes 4194320 | tf_op jit(solution)/shard_map/psum | solution.py:12
  452.6 6.2 %multiply_reduce_fusion = f32[2048]{0:T(1024)S(1)} fusion(f32[2048,1024]{1,0:T(8,128)} %all-reduce.4.cloned.1.call-done, f32[1024]{0:T(1024)S(1)} %broadcast_multiply_fusion, f32[1024]{0:T(1024)S(1)} %copy-done.10, f32[2048]{0:T(1024)S(1)} %bitcast.30, f32[2048]{0:T(1024)S(1)} %add_rsqrt_fusion, bf16[2048,512]{1,0:T(8,128)(2,1)} %get-tuple-element.2, ...), kind=kLoop, calls=%fused_computation.5 | loop fusion | flops 23066624 | bytes 12615680 | tf_op jit(solution)/shard_map/reduce_sum | solution.py:93
  458.8 14.6 %psum.39 = f32[2048]{0:T(1024)S(1)} all-reduce(f32[2048]{0:T(1024)S(1)} %multiply_reduce_fusion), channel_id=1, replica_groups=mesh['replica'=8,'tensor'=16] {'replica'}, use_global_device_ids=true, to_apply=%region_7.8 | all-reduce | flops 2048 | bytes 16384 | tf_op jit(solution)/shard_map/psum | solution.py:93
  473.4 0.0 copy-start.1
  473.4 29.1 %subtract_convert_fusion = bf16[3,512,1024]{2,1,0:T(8,128)(2,1)} fusion(f32[3,512,1024]{2,1,0:T(8,128)} %param.22, bf16[2048,3,512]{0,2,1:T(8,128)(2,1)} %bitcast.26, f32[2048,1024]{1,0:T(8,128)} %all-reduce.4.cloned.1.call-done, f32[2048]{0:T(1024)S(1)} %fusion.13, f32[1024]{0:T(1024)S(1)} %broadcast_multiply_fusion, f32[1024]{0:T(1024)S(1)} %copy-done.10, ...), kind=kOutput, calls=%fused_computation.9 | convolution fusion | flops 38684590080 | bytes 28344320 | tf_op jit(solution)/shard_map/zag,zh->agh/dot_general | solution.py:95
  (25 shorter events, 0.1 us)
Async XLA Ops:
  7.2 9.1 %copy-start = (bf16[2,128,896]{2,1,0:T(8,128)(2,1)S(1)}, bf16[2,128,896]{2,1,0:T(8,128)(2,1)}, u32[]{:S(2)}) copy-start(bf16[2,128,896]{2,1,0:T(8,128)(2,1)} %param.12) | copy-start | bytes 1376260
  7.2 104.1 %reduce-scatter.2.cloned.1.call-start = ((), (), s32[]{:S(2)}) async-start(), calls=%async_computation.1 | async-start | bytes 8912896 | tf_op jit(solution)/shard_map/reduce_scatter | solution.py:41
  23.4 89.2 %copy-start.4 = (bf16[2,128,512]{2,1,0:T(8,128)(2,1)S(1)}, bf16[2,128,512]{2,1,0:T(8,128)(2,1)}, u32[]{:S(2)}) copy-start(bf16[2,128,512]{2,1,0:T(8,128)(2,1)} %param.15) | copy-start | bytes 786436
  23.4 89.3 %copy-start.5 = (bf16[128,512]{1,0:T(8,128)(2,1)S(1)}, bf16[128,512]{1,0:T(8,128)(2,1)}, u32[]{:S(2)}) copy-start(bf16[128,512]{1,0:T(8,128)(2,1)} %param.17) | copy-start | bytes 393220
  23.4 89.3 %copy-start.6 = (bf16[128,512]{1,0:T(8,128)(2,1)S(1)}, bf16[128,512]{1,0:T(8,128)(2,1)}, u32[]{:S(2)}) copy-start(bf16[128,512]{1,0:T(8,128)(2,1)} %param.16) | copy-start | bytes 393220
  23.4 89.3 %copy-start.7 = (bf16[128,512]{1,0:T(8,128)(2,1)S(1)}, bf16[128,512]{1,0:T(8,128)(2,1)}, u32[]{:S(2)}) copy-start(bf16[128,512]{1,0:T(8,128)(2,1)} %param.20) | copy-start | bytes 393220
  23.4 89.3 %copy-start.8 = (bf16[128,512]{1,0:T(8,128)(2,1)S(1)}, bf16[128,512]{1,0:T(8,128)(2,1)}, u32[]{:S(2)}) copy-start(bf16[128,512]{1,0:T(8,128)(2,1)} %param.19) | copy-start | bytes 393220
  23.4 89.3 %copy-start.9 = (bf16[128,512]{1,0:T(8,128)(2,1)S(1)}, bf16[128,512]{1,0:T(8,128)(2,1)}, u32[]{:S(2)}) copy-start(bf16[128,512]{1,0:T(8,128)(2,1)} %param.18) | copy-start | bytes 393220
  23.4 139.4 %all-gather.3.cloned.1.call-start = ((), (), s32[]{:S(2)}) async-start(), calls=%async_computation.2 | async-start | bytes 9437184 | tf_op jit(solution)/shard_map/all_gather | solution.py:64
  112.6 64.7 %copy-start.3 = (bf16[2,128,512]{2,1,0:T(8,128)(2,1)}, bf16[2,128,512]{2,1,0:T(8,128)(2,1)S(1)}, u32[]{:S(2)}) copy-start(bf16[2,128,512]{2,1,0:T(8,128)(2,1)S(1)} %add_convert_fusion) | copy-start | bytes 786436
  113.9 231.8 %all-reduce.4.cloned.1.call-start = ((), (), s32[]{:S(2)}) async-start(), calls=%async_computation.3 | async-start | bytes 16777216 | tf_op jit(solution)/shard_map/psum | solution.py:86
  203.4 4.0 copy-start.11
  203.4 12.8 %copy-start.10 = (f32[1024]{0:T(1024)S(1)}, f32[1024]{0:T(1024)}, u32[]{:S(2)}) copy-start(f32[1024]{0:T(1024)} %param.23) | copy-start | bytes 12292
  203.4 249.1 %all-reduce.6.cloned.1.call-start = ((), (), s32[]{:S(2)}) async-start(), calls=%async_computation.4 | async-start | bytes 8388608 | tf_op jit(solution)/shard_map/psum | solution.py:12
  452.6 20.8 %copy-start.2 = (bf16[2048,512]{1,0:T(8,128)(2,1)S(1)}, bf16[2048,512]{1,0:T(8,128)(2,1)}, u32[]{:S(2)}) copy-start(bf16[2048,512]{1,0:T(8,128)(2,1)} %get-tuple-element.2) | copy-start | bytes 6291460
  473.4 29.1 %copy-start.1 = (bf16[2,128,896]{2,1,0:T(8,128)(2,1)S(1)}, bf16[2,128,896]{2,1,0:T(8,128)(2,1)}, u32[]{:S(2)}) copy-start(bf16[2,128,896]{2,1,0:T(8,128)(2,1)} %param.12) | copy-start | bytes 1376260
Sparse Core Ops, SparseCore 0:
  23.6 87.6 reduce-scatter.1
  114.0 48.8 all-gather.2
  203.6 142.0 all-reduce.3
  349.9 102.5 all-reduce.5
where the time goes:
time: 510 us; the launch traced here: 509 us
  waiting for transfers between devices  354 us (69%)
  matrix products  62.2 us (12%)
  blocking collectives  38.1 us (7%)
  other arithmetic  24.3 us (5%)
  local copies, waits for them, and re-layouts  15.8 us (3%)
  between operations  14 us (3%)
    psum x1, waiting for transfers between devices, body(): drafted = lax.psum(partial_result, 'tensor')  129 us
    psum x1, waiting for transfers between devices, spread(): return lax.psum(jnp.where(mine, array, jnp.zeros_like(array)), axis)  88.2 us
    reduce_scatter x1, waiting for transfers between devices, body(): lax.psum_scatter(lax.dot_general(columns, tokens, (((0,), (1,)), ((), ())...  87.8 us
    all_gather x1, waiting for transfers between devices, body(): lax.all_gather(payload, 'replica', axis=0, tiled=True)  48.8 us
    dot_general x1, matrix products, body(): jnp.einsum('zag,zh->agh', input_rows, loss_gradient, precision=lax.Precis...  29.1 us
    dot_general x1, matrix products, body(): jnp.einsum('wmg,mgf->wf', input_rows, draft_input_weight, precision=lax.P...  26.1 us
    psum x1, blocking collectives, body(): squares = lax.psum(jnp.sum(drafted * drafted, axis=1), 'replica')  14.7 us
    psum x1, blocking collectives, body(): inner = lax.psum(jnp.sum(error * drafted, axis=1), 'replica')  14.6 us
  transfers between devices with their start and end apart: 4, of which 4 were waited for; matrix products, arithmetic and copies ran while one was open for 2% of the time, Pallas kernels for 0%

commit v1 on v0

v1 whole, which is shorter than its diff:
```python
import functools

import jax
import jax.numpy as jnp
from jax import lax
from jax.experimental import pallas as pl
from jax.experimental.pallas import tpu as pltpu
from jax.sharding import PartitionSpec as P

step_rate = 8.0
epsilon = 1e-06
side = 4
cores = 2
block_units = 32
f32 = jnp.float32
bf16 = jnp.bfloat16
mesh_axes = ("replica", "tensor")
vmem = 56 * 1024 * 1024


def coordinates(device):
    replica, tensor = divmod(device, side * side)
    x, c = divmod(replica, cores)
    z, y = divmod(tensor, side)
    return x, c, z, y


def device_at(x, c, z, y):
    return ((x % side) * cores + c % cores) * side * side + (z % side) * side + y % side


def moved(target):
    return [(d, target(*coordinates(d))) for d in range(side * cores * side * side)]


def along_first(shift):
    return moved(
        lambda x, c, z, y: device_at(x, c, z + shift * (c == 0), y + shift * (c == 1))
    )


def along_second(shift):
    return moved(
        lambda x, c, z, y: device_at(x, c, z + shift * (c == 1), y + shift * (c == 0))
    )


def along_x(shift):
    return moved(lambda x, c, z, y: device_at(x + shift, c, z, y))


def other_core():
    return moved(lambda x, c, z, y: device_at(x, 1 - c, z, y))


def send(array, pairs):
    return lax.ppermute(array, mesh_axes, pairs)


def plus(*terms):
    return functools.reduce(jnp.add, [term.astype(f32) for term in terms])


def relative_tables():
    replica, tensor = lax.axis_index("replica"), lax.axis_index("tensor")
    x, c = replica // cores, replica % cores
    z, y = tensor // side, tensor % side
    step = jnp.arange(side * side, dtype=jnp.int32)
    first, second = step // side, step % side
    zs = (z + jnp.where(c == 0, first, second)) % side
    ys = (y + jnp.where(c == 0, second, first)) % side
    block = zs * side + ys
    late = jnp.where(ys // cores == c, 0, side) + (zs - x) % side
    return block.astype(jnp.int32), late.astype(jnp.int32)


def piece_specs(rows, columns):
    def spec(k):
        return pl.BlockSpec(
            (1, rows, columns), lambda i, *tables: (jnp.clip(i - 2 * k, 0, 1), 0, 0)
        )

    return [spec(k) for k in range(8)]


def piece_shapes(rows, columns):
    return [jax.ShapeDtypeStruct((2, rows, columns), bf16)] * 8


def store_piece(i, value, pieces):
    for k in range(8):

        @pl.when(i // 2 == k)
        def _():
            pieces[k][0] = value


def down_kernel(block_ref, tokens_ref, coded_ref, exponent_ref, *pieces):
    i = pl.program_id(0)
    units, columns = coded_ref.shape
    factor = jnp.exp2(exponent_ref[...].astype(f32) - 127.0).astype(bf16)
    weight = coded_ref[...].reshape(units // block_units, block_units, columns)
    weight = (weight * factor[:, None, :]).reshape(units, columns)
    total = jnp.dot(tokens_ref[...], weight, preferred_element_type=f32)
    store_piece(i, total.astype(bf16), pieces)


def down_pieces(block, tokens, coded_weight, block_exponent):
    rows, units = tokens.shape
    width = coded_weight.shape[1] // (side * side)
    return pl.pallas_call(
        down_kernel,
        grid_spec=pltpu.PrefetchScalarGridSpec(
            num_scalar_prefetch=1,
            grid=(side * side,),
            in_specs=[
                pl.BlockSpec((rows, units), lambda i, block: (0, 0)),
                pl.BlockSpec((units, width), lambda i, block: (0, block[i])),
                pl.BlockSpec((units // block_units, width), lambda i, block: (0, block[i])),
            ],
            out_specs=piece_specs(rows, width),
        ),
        out_shape=piece_shapes(rows, width),
        compiler_params=pltpu.CompilerParams(vmem_limit_bytes=vmem),
        name="down_projection",
    )(block, tokens, coded_weight, block_exponent)


def early_kernel(block_ref, pair_ref, third_ref, weight_ref, early_ref, features_ref):
    i = pl.program_id(0)
    width = third_ref.shape[2]
    layers = pair_ref[0]
    features_ref[0] = layers
    early_ref[0] = jnp.dot(
        layers[:, :width], weight_ref[0], preferred_element_type=f32
    ) + jnp.dot(layers[:, width:], weight_ref[1], preferred_element_type=f32)

    @pl.when(block_ref[i] % 2 == 0)
    def _():
        early_ref[0] += jnp.dot(third_ref[0], weight_ref[2], preferred_element_type=f32)


def early_projection(block, gathered, weight):
    replicas, slots, _ = gathered.shape
    layers, width, columns = weight.shape
    blocks = side * side
    return pl.pallas_call(
        early_kernel,
        grid_spec=pltpu.PrefetchScalarGridSpec(
            num_scalar_prefetch=1,
            grid=(blocks,),
            in_specs=[
                pl.BlockSpec(
                    (1, slots, 2 * width), lambda i, block: (block[i] // 2, 0, block[i] % 2)
                ),
                pl.BlockSpec((1, slots, width), lambda i, block: (block[i] // 2, 0, 4)),
                pl.BlockSpec((layers, width, columns), lambda i, block: (0, 0, 0)),
            ],
            out_specs=[
                pl.BlockSpec((1, slots, columns), lambda i, block: (i, 0, 0)),
                pl.BlockSpec((1, slots, 2 * width), lambda i, block: (i, 0, 0)),
            ],
        ),
        out_shape=[
            jax.ShapeDtypeStruct((blocks, slots, columns), f32),
            jax.ShapeDtypeStruct((blocks, slots, layers * width), bf16),
        ],
        compiler_params=pltpu.CompilerParams(vmem_limit_bytes=vmem),
        name="early_projection",
    )(block, gathered, gathered, weight)


def late_kernel(
    block_ref, late_ref, early_ref, third_ref, late_third_ref, weight_ref, _, features_ref, *pieces
):
    i = pl.program_id(0)
    is_late = block_ref[i] % 2 == 1

    @pl.when(is_late)
    def _():
        features_ref[0] = late_third_ref[0]
        total = early_ref[0] + jnp.dot(
            late_third_ref[0], weight_ref[0], preferred_element_type=f32
        )
        store_piece(i, total.astype(bf16), pieces)

    @pl.when(jnp.logical_not(is_late))
    def _():
        features_ref[0] = third_ref[0]
        store_piece(i, early_ref[0].astype(bf16), pieces)


def late_projection(block, late, early, gathered, late_third, weight, features):
    blocks, slots, columns = early.shape
    layers, width, _ = weight.shape
    outs = pl.pallas_call(
        late_kernel,
        grid_spec=pltpu.PrefetchScalarGridSpec(
            num_scalar_prefetch=2,
            grid=(blocks,),
            in_specs=[
                pl.BlockSpec((1, slots, columns), lambda i, block, late: (i, 0, 0)),
                pl.BlockSpec((1, slots, width), lambda i, block, late: (block[i] // 2, 0, 4)),
                pl.BlockSpec((1, slots, width), lambda i, block, late: (late[i], 0, 0)),
                pl.BlockSpec((1, width, columns), lambda i, block, late: (2, 0, 0)),
                pl.BlockSpec(memory_space=pl.ANY),
            ],
            out_specs=[pl.BlockSpec((1, slots, width), lambda i, block, late: (i, 0, 2))]
            + piece_specs(slots, columns),
        ),
        out_shape=[jax.ShapeDtypeStruct(features.shape, bf16)] + piece_shapes(slots, columns),
        input_output_aliases={6: 0},
        compiler_params=pltpu.CompilerParams(vmem_limit_bytes=vmem),
        name="late_projection",
    )(block, late, early, gathered, late_third, weight, features)
    return outs[0], outs[1:]


def reduce_blocks(pieces):
    rows = pieces[0].shape[1]
    half = rows // 2
    near_right = send(pieces[4], along_first(1))
    near_left = send(pieces[5], along_first(-1))
    direct_right = send(pieces[3], along_first(1))
    direct_left = send(pieces[6], along_first(-1))
    far_right = send(plus(pieces[2], near_right).astype(bf16), along_first(1))
    far_left = send(plus(pieces[7], near_left).astype(bf16), along_first(-1))
    low = plus(pieces[0], far_right, direct_left)
    high = plus(pieces[1], far_left, direct_right)
    own, next_one, opposite, last_one = low[0], low[1], high[0], high[1]
    near_right = send(opposite[:half].astype(bf16), along_second(1))
    near_left = send(opposite[half:].astype(bf16), along_second(-1))
    right = jnp.concatenate([next_one[:half] + near_right.astype(f32), next_one[half:]])
    left = jnp.concatenate([last_one[:half], last_one[half:] + near_left.astype(f32)])
    from_left = send(right.astype(bf16), along_second(1))
    from_right = send(left.astype(bf16), along_second(-1))
    return plus(own, from_left, from_right)


def gather_ring(own, along):
    half = own.shape[0] // 2
    previous = send(own, along(1))
    following = send(own, along(-1))
    opposite_low = send(previous[:half], along(1))
    opposite_high = send(following[half:], along(-1))
    return [own, following, opposite_low, opposite_high, previous]


def body(
    gated_hidden,
    coded_weight,
    block_exponent,
    stream_input,
    lower_layer,
    middle_layer,
    prior_lower,
    prior_middle,
    prior_upper,
    accepted,
    draft_input_weight,
    draft_gain,
):
    steps, rows, unit_count = gated_hidden.shape
    feature_slice = stream_input.shape[2]
    out_slice = draft_input_weight.shape[2]
    replicas = lax.axis_size("replica")
    tensors = lax.axis_size("tensor")
    width = feature_slice * tensors
    slots_all = steps * rows * replicas
    slots = rows * 3 // 4
    block, late = relative_tables()

    with jax.named_scope("down"):
        pieces = down_pieces(
            block, gated_hidden.reshape(steps * rows, unit_count), coded_weight, block_exponent
        )

    with jax.named_scope("select"):
        place = jnp.arange(rows, dtype=jnp.int32)
        before = place[:, None] <= place[None, :]
        first_live = (accepted >= 1).astype(jnp.int32)
        second_live = (accepted >= 2).astype(jnp.int32)
        first_slot = jnp.sum(jnp.where(before, first_live[:, None], 0), axis=0) - 1
        second_slot = 2 * slots - jnp.sum(jnp.where(before, second_live[:, None], 0), axis=0)
        first_slot = jnp.where(first_live == 1, first_slot, -1)
        second_slot = jnp.where(second_live == 1, second_slot, -1)
        slot = jnp.arange(2 * slots, dtype=jnp.int32)[:, None]
        select = (slot == jnp.concatenate([first_slot, second_slot])[None, :]).astype(bf16)

        def pick(chosen, first, second):
            return jnp.dot(
                chosen, jnp.concatenate([first, second]), preferred_element_type=f32
            ).astype(bf16)

        layers = pick(
            select,
            jnp.concatenate([prior_lower, prior_middle], axis=1),
            jnp.concatenate([lower_layer, middle_layer], axis=1),
        )
        third = jnp.dot(
            select[:slots, :rows], prior_upper, preferred_element_type=f32
        ).astype(bf16)
        payload = jnp.concatenate([layers[:slots], layers[slots:], third], axis=1)
    gathered = lax.all_gather(payload, "replica", axis=0, tiled=False)
    weight = draft_input_weight.astype(bf16)

    with jax.named_scope("early"):
        early, features = early_projection(block, gathered, weight)

    with jax.named_scope("reduce_down"):
        summed = reduce_blocks(pieces)
    upper_rows = (
        stream_input.astype(f32) + summed.reshape(steps, rows, feature_slice)
    ).astype(bf16)
    upper_layer = upper_rows

    with jax.named_scope("late"):
        third = pick(select[slots:], prior_upper, upper_rows[0])
        near = [third] + [send(third, along_x(-shift)) for shift in (1, 2, 3)]
        near = jnp.stack(near)
        late_third = jnp.concatenate([near, send(near, other_core())])
        features, pieces = late_projection(
            block, late, early, gathered, late_third, weight, features
        )

    with jax.named_scope("targets"):
        chosen = pick(select, upper_rows[0], upper_rows[1])
        parity = lax.axis_index("tensor") % 2
        even, odd = chosen[:slots], chosen[slots:]
        got = []
        for turn in range(2):
            pairs = []
            for d in range(replicas * tensors):
                r, t = divmod(d, tensors)
                pairs.append((d, (t // 2) * tensors + 2 * r + (t + turn) % 2))
            got.append(send(jnp.where((parity + turn) % 2 == 0, even, odd), pairs))
        targets = jnp.concatenate(
            [jnp.where(parity == 0, got[0], got[1]), jnp.where(parity == 0, got[1], got[0])],
            axis=1,
        ).astype(f32)

    with jax.named_scope("reduce_draft"):
        drafted = reduce_blocks(pieces)

    with jax.named_scope("norm"):
        gain = draft_gain[None, :]
        scaled = gain * drafted
        sums = jnp.stack(
            [
                jnp.sum(drafted * drafted, axis=1),
                jnp.sum(scaled * scaled, axis=1),
                jnp.sum(scaled * targets, axis=1),
            ]
        )
        sums = sums + send(sums, other_core())
        sums = sums + send(sums, along_x(1)) + send(sums, along_x(2)) + send(sums, along_x(3))
        scale = lax.rsqrt(sums[0] / width + epsilon)
        inner = (scale * sums[1] - sums[2]) / slots_all
        error = gain * (scaled * scale[:, None] - targets) / slots_all
        slope = (scale[:, None] * error - drafted * (scale**3 * inner / width)[:, None]).astype(
            bf16
        )

    with jax.named_scope("gather_slope"):
        ring = jnp.concatenate(gather_ring(slope, along_second))
        slopes = jnp.concatenate(gather_ring(ring, along_first))

    with jax.named_scope("step"):
        inputs = features.reshape(-1, 3, feature_slice)
        update_step = jnp.einsum("zag,zh->agh", inputs, slopes, preferred_element_type=f32)
        new_weight = (draft_input_weight - step_rate * update_step).astype(bf16)
    return (upper_layer, new_weight)


def solution(mesh):
    return jax.shard_map(
        body,
        mesh=mesh,
        in_specs=(
            P(None, "replica", "tensor"),
            P("tensor", None),
            P("tensor", None),
            P(None, "replica", "tensor"),
            P("replica", "tensor"),
            P("replica", "tensor"),
            P("replica", "tensor"),
            P("replica", "tensor"),
            P("replica", "tensor"),
            P("replica"),
            P(None, "tensor", "replica"),
            P("replica"),
        ),
        out_specs=(P(None, "replica", "tensor"), P(None, "tensor", "replica")),
        check_vma=False,
    )
```

time: 510 us -> 239 us (0.47)
  waiting for transfers between devices: 354 us -> 61.5 us
  starting transfers between devices: 0.35 us -> 62.5 us
  Pallas kernels: 0 us -> 52 us
  matrix products: 62.2 us -> 13.1 us
  blocking collectives: 38.1 us -> 0 us
  other arithmetic: 24.3 us -> 14.8 us
    psum x2 -> x0, waiting for transfers between devices: 218 us -> none  [the longest x1 129 us: body(): drafted = lax.psum(partial_result, 'tensor')]
    reduce_scatter x1 -> x0, waiting for transfers between devices: 87.8 us -> none  [body(): lax.psum_scatter(lax.dot_general(columns, tokens, (((0,), (1,)), ((), ())...]
    ppermute x0 -> x38, starting transfers between devices: none -> 62.5 us  [send(): return lax.ppermute(array, mesh_axes, pairs)]
    ppermute x0 -> x38, waiting for transfers between devices: none -> 61.4 us  [send(): return lax.ppermute(array, mesh_axes, pairs)]
    pallas_call x0 -> x3, Pallas kernels: none -> 52 us  [the longest x1 18.8 us: early_projection(): pl.pallas_call(early_kernel, grid_spec=pltpu.PrefetchScalarGridSpec(num_s...]
    dot_general x3 -> x5, matrix products: 62.2 us -> 13.1 us  [the longest x1 10.3 us: body(): jnp.einsum('zag,zh->agh', inputs, slopes, preferred_element_type=f32)]
    all_gather x1, waiting for transfers between devices: 48.8 us -> 0.02 us  [body(): gathered = lax.all_gather(payload, 'replica', axis=0, tiled=False)]
    psum x2 -> x0, blocking collectives: 29.3 us -> none  [the longest x1 14.7 us: body(): squares = lax.psum(jnp.sum(drafted * drafted, axis=1), 'replica')]
  transfers between devices with their start and end apart: 4 -> 39, of which waited for: 4 -> 20; matrix products, arithmetic and copies ran while one was open for 2% -> 12% of each run, Pallas kernels for 0% -> 8%
where the time goes in v1:
time: 239 us; the launch traced here: 238 us
  starting transfers between devices  62.5 us (26%)
  waiting for transfers between devices  61.5 us (26%)
  Pallas kernels  52 us (22%)
  local copies, waits for them, and re-layouts  19.1 us (8%)
  other arithmetic  14.8 us (6%)
  between operations  14.6 us (6%)
  matrix products  13.1 us (5%)
    ppermute x38, starting transfers between devices, send(): return lax.ppermute(array, mesh_axes, pairs)  62.5 us
    ppermute x38, waiting for transfers between devices, send(): return lax.ppermute(array, mesh_axes, pairs)  61.4 us
    pallas_call x1, Pallas kernels, early_projection(): pl.pallas_call(early_kernel, grid_spec=pltpu.PrefetchScalarGridSpec(num_s...  18.8 us
    pallas_call x1, Pallas kernels, down_pieces(): pl.pallas_call(down_kernel, grid_spec=pltpu.PrefetchScalarGridSpec(num_sc...  18.1 us
    pallas_call x1, Pallas kernels, late_projection(): pl.pallas_call(late_kernel, grid_spec=pltpu.PrefetchScalarGridSpec(num_sc...  15.1 us
    reshape x1, local copies, waits for them, and re-layouts, body(): inputs = features.reshape(-1, 3, feature_slice)  11.9 us
    dot_general x1, matrix products, body(): jnp.einsum('zag,zh->agh', inputs, slopes, preferred_element_type=f32)  10.3 us
    unnamed x28, local copies, waits for them, and re-layouts  5.33 us
  transfers between devices with their start and end apart: 39, of which 20 were waited for; matrix products, arithmetic and copies ran while one was open for 12% of the time, Pallas kernels for 8%

profile of v1, /device:TPU:0, one launch (start us, length us, event | category | flops | bytes accessed | tf_op | source)
XLA Modules:
  0.0 237.6 jit_solution(16001285577792675834)
XLA Ops:
  12.7 18.1 %down_projection.1 = (bf16[2,256,512]{2,1,0:T(8,128)(2,1)}, bf16[2,256,512]{2,1,0:T(8,128)(2,1)}, bf16[2,256,512]{2,1,0:T(8,128)(2,1)}, bf16[2,256,512]{2,1,0:T(...) custom-call(s32[16]{0:T(128)} %multiply_add_fusion.block_ref, ...), custom_call_target="tpu_custom_call" | custom-call | tf_op jit(solution)/shard_map/down/down_projection/pallas_call | solution.py:111
  30.8 4.3 %collective-permute-start.3 = (bf16[2,256,512]{2,1,0:T(8,128)(2,1)}, bf16[2,256,512]{2,1,0:T(8,128)(2,1)S(1)}, u32[]{:S(2)}, u32[]{:S(2)}) collective-permute-start(bf16[2,256,512]{2,1,0:T(8,128)(2,1)} %get-tuple-element.27), channel_id=1, source_target_pairs={{0,12},{1,13},{2,14},{3,15},{4,0},{5,1},{6,2},{7,3},{8,4},{9,5},{1... | collective-permute-start | bytes 1572872 | tf_op jit(solution)/shard_map/reduce_down/ppermute | solution.py:57
  35.1 7.0 %collective-permute-done.3 = bf16[2,256,512]{2,1,0:T(8,128)(2,1)S(1)} collective-permute-done((bf16[2,256,512]{2,1,0:T(8,128)(2,1)}, bf16[2,256,512]{2,1,0:T(8,128)(2,1)S(1)}, u32[]{:S(2)}, u32[]{:S(2)}) %collective-permute-start.3) | collective-permute-done | bytes 524320 | tf_op jit(solution)/shard_map/reduce_down/ppermute | solution.py:57
  43.3 3.7 %collective-permute-start.4 = (bf16[2,256,512]{2,1,0:T(8,128)(2,1)S(1)}, bf16[2,256,512]{2,1,0:T(8,128)(2,1)S(1)}, u32[]{:S(2)}, u32[]{:S(2)}) collective-permute-start(bf16[2,256,512]{2,1,0:T(8,128)(2,1)S(1)} %add_convert_fusion), channel_id=1, source_target_pairs={{0,12},{1,13},{2,14},{3,15},{4,0},{5,1},{6,2},{7,3},{8,4},{9,5},{1... | collective-permute-start | bytes 1572872 | tf_op jit(solution)/shard_map/reduce_down/ppermute | solution.py:57
  48.2 2.0 collective-permute-start.1
  51.3 2.3 collective-permute-done.4
  57.2 3.5 %collective-permute-done.2 = bf16[2,256,512]{2,1,0:T(8,128)(2,1)S(1)} collective-permute-done((bf16[2,256,512]{2,1,0:T(8,128)(2,1)}, bf16[2,256,512]{2,1,0:T(8,128)(2,1)S(1)}, u32[]{:S(2)}, u32[]{:S(2)}) %collective-permute-start.2) | collective-permute-done | bytes 524320 | tf_op jit(solution)/shard_map/reduce_down/ppermute | solution.py:57
  61.1 3.0 %collective-permute-start.9 = (bf16[256,512]{1,0:T(8,128)(2,1)S(1)}, bf16[256,512]{1,0:T(8,128)(2,1)S(1)}, u32[]{:S(2)}, u32[]{:S(2)}) collective-permute-start(bf16[256,512]{1,0:T(8,128)(2,1)S(1)} %pad_maximum_fusion.3), channel_id=1, source_target_pairs={{0,3},{1,0},{2,1},{3,2},{4,7},{5,4},{6,5},{7,6},{8,11},{9,8},{10,9... | collective-permute-start | bytes 786440 | tf_op jit(solution)/shard_map/reduce_down/ppermute | solution.py:57
  64.3 5.0 %convert_element_type.177.weight_ref = bf16[3,512,1024]{2,1,0:T(8,128)(2,1)} convert(f32[3,512,1024]{2,1,0:T(8,128)} %param.22) | non-fusion elementwise | flops 1572864 | bytes 9437184 | tf_op jit(solution)/shard_map/convert_element_type | solution.py:305
  69.3 2.5 %collective-permute-done.7 = bf16[256,512]{1,0:T(8,128)(2,1)S(1)} collective-permute-done((bf16[256,512]{1,0:T(8,128)(2,1)S(1)}, bf16[256,512]{1,0:T(8,128)(2,1)S(1)}, u32[]{:S(2)}, u32[]{:S(2)}) %collective-permute-start.7) | collective-permute-done | bytes 262176 | tf_op jit(solution)/shard_map/reduce_down/ppermute | solution.py:57
  73.9 2.7 %collective-permute-start.11 = (bf16[96,512]{1,0:T(8,128)(2,1)S(1)}, bf16[96,512]{1,0:T(8,128)(2,1)S(1)}, u32[]{:S(2)}, u32[]{:S(2)}) collective-permute-start(bf16[96,512]{1,0:T(8,128)(2,1)S(1)} %get-tuple-element.79), channel_id=1, source_target_pairs={{0,64},{1,65},{2,66},{3,67},{4,68},{5,69},{6,70},{7,71},{8,72},{9,... | collective-permute-start | bytes 294920 | tf_op jit(solution)/shard_map/late/ppermute | solution.py:57
  83.1 18.8 %early_projection.1 = (f32[16,96,1024]{2,1,0:T(8,128)}, bf16[16,96,1536]{2,1,0:T(8,128)(2,1)}) custom-call(s32[16]{0:T(128)} %multiply_add_fusion.block_ref, bf16[8,96,2560]{2,1,0:T(8,128)(2,1)} %bitcast.94, bf16[8,96,2560]{2,1,0:T(8,128)(2,1)} %bitcast.95, bf16[3,512,1024]{2,1,0:T(8,128)(2,1)} %convert_element_type.177.weight_ref), custom_call_target="tpu_custom_call" | custom-call | tf_op jit(solution)/shard_map/early/early_projection/pallas_call | solution.py:147
  101.8 15.1 %late_projection.1 = (bf16[16,96,1536]{2,1,0:T(8,128)(2,1)}, bf16[2,96,1024]{2,1,0:T(8,128)(2,1)}, bf16[2,96,1024]{2,1,0:T(8,128)(2,1)}, bf16[2,96,1024]{2,1,0:T...) custom-call(s32[16]{0:T(128)} %multiply_add_fusion.block_ref, ...), custom_call_target="tpu_custom_call", output_to_operand_aliasing={{0}: (6, {})} | custom-call | tf_op jit(solution)/shard_map/late/late_projection/pallas_call | solution.py:196
  116.9 3.7 %collective-permute-start.17 = (bf16[2,96,1024]{2,1,0:T(8,128)(2,1)}, bf16[2,96,1024]{2,1,0:T(8,128)(2,1)S(1)}, u32[]{:S(2)}, u32[]{:S(2)}) collective-permute-start(bf16[2,96,1024]{2,1,0:T(8,128)(2,1)} %get-tuple-element.38), channel_id=1, source_target_pairs={{0,12},{1,13},{2,14},{3,15},{4,0},{5,1},{6,2},{7,3},{8,4},{9,5},{1... | collective-permute-start | bytes 1179656 | tf_op jit(solution)/shard_map/reduce_draft/ppermute | solution.py:57
  120.9 5.2 %collective-permute-done.17 = bf16[2,96,1024]{2,1,0:T(8,128)(2,1)S(1)} collective-permute-done((bf16[2,96,1024]{2,1,0:T(8,128)(2,1)}, bf16[2,96,1024]{2,1,0:T(8,128)(2,1)S(1)}, u32[]{:S(2)}, u32[]{:S(2)}) %collective-permute-start.17) | collective-permute-done | bytes 393248 | tf_op jit(solution)/shard_map/reduce_draft/ppermute | solution.py:57
  127.3 3.7 %collective-permute-start.18 = (bf16[2,96,1024]{2,1,0:T(8,128)(2,1)S(1)}, bf16[2,96,1024]{2,1,0:T(8,128)(2,1)S(1)}, u32[]{:S(2)}, u32[]{:S(2)}) collective-permute-start(bf16[2,96,1024]{2,1,0:T(8,128)(2,1)S(1)} %add_convert_fusion.2), channel_id=1, source_target_pairs={{0,12},{1,13},{2,14},{3,15},{4,0},{5,1},{6,2},{7,3},{8,4},{9,5},{1... | collective-permute-start | bytes 1179656 | tf_op jit(solution)/shard_map/reduce_draft/ppermute | solution.py:57
  131.8 6.9 %collective-permute-start.16 = (bf16[2,96,1024]{2,1,0:T(8,128)(2,1)}, bf16[2,96,1024]{2,1,0:T(8,128)(2,1)S(1)}, u32[]{:S(2)}, u32[]{:S(2)}) collective-permute-start(bf16[2,96,1024]{2,1,0:T(8,128)(2,1)} %get-tuple-element.35), channel_id=1, source_target_pairs={{0,12},{1,13},{2,14},{3,15},{4,0},{5,1},{6,2},{7,3},{8,4},{9,5},{1... | collective-permute-start | bytes 1179656 | tf_op jit(solution)/shard_map/reduce_draft/ppermute | solution.py:57
  140.1 1.9 collective-permute-start.22
  142.1 5.5 %collective-permute-done.16 = bf16[2,96,1024]{2,1,0:T(8,128)(2,1)S(1)} collective-permute-done((bf16[2,96,1024]{2,1,0:T(8,128)(2,1)}, bf16[2,96,1024]{2,1,0:T(8,128)(2,1)S(1)}, u32[]{:S(2)}, u32[]{:S(2)}) %collective-permute-start.16) | collective-permute-done | bytes 393248 | tf_op jit(solution)/shard_map/reduce_draft/ppermute | solution.py:57
  150.4 2.1 collective-permute-start.23
  152.5 2.5 %collective-permute-done.20 = bf16[48,1024]{1,0:T(8,128)(2,1)S(1)} collective-permute-done((bf16[48,1024]{1,0:T(8,128)(2,1)S(1)}, bf16[48,1024]{1,0:T(8,128)(2,1)S(1)}, u32[]{:S(2)}, u32[]{:S(2)}) %collective-permute-start.20) | collective-permute-done | bytes 98336 | tf_op jit(solution)/shard_map/reduce_draft/ppermute | solution.py:57
  156.1 5.8 %collective-permute-done.21 = bf16[96,1024]{1,0:T(8,128)(2,1)S(1)} collective-permute-done((bf16[96,1024]{1,0:T(8,128)(2,1)S(1)}, bf16[96,1024]{1,0:T(8,128)(2,1)S(1)}, u32[]{:S(2)}, u32[]{:S(2)}) %collective-permute-start.21) | collective-permute-done | bytes 196640 | tf_op jit(solution)/shard_map/reduce_draft/ppermute | solution.py:57
  163.4 4.3 %collective-permute-start.28 = (f32[3,96]{1,0:T(4,128)S(1)}, f32[3,96]{1,0:T(4,128)S(1)}, u32[]{:S(2)}, u32[]{:S(2)}) collective-permute-start(f32[3,96]{1,0:T(4,128)S(1)} %fusion.55), channel_id=1, source_target_pairs={{0,64},{1,65},{2,66},{3,67},{4,68},{5,69},{6,70},{7,71},{8,72},{9,... | collective-permute-start | bytes 3464 | tf_op jit(solution)/shard_map/norm/ppermute | solution.py:57
  171.4 1.9 collective-permute-done.27
  173.6 3.2 %collective-permute-start.30 = (bf16[96,1024]{1,0:T(8,128)(2,1)S(1)}, bf16[96,1024]{1,0:T(8,128)(2,1)S(1)}, u32[]{:S(2)}, u32[]{:S(2)}) collective-permute-start(bf16[96,1024]{1,0:T(8,128)(2,1)S(1)} %get-tuple-element.44), channel_id=1, source_target_pairs={{0,3},{1,0},{2,1},{3,2},{4,7},{5,4},{6,5},{7,6},{8,11},{9,8},{10,9... | collective-permute-start | bytes 589832 | tf_op jit(solution)/shard_map/gather_slope/ppermute | solution.py:57
  177.5 3.0 %collective-permute-done.31 = bf16[96,1024]{1,0:T(8,128)(2,1)S(1)} collective-permute-done((bf16[96,1024]{1,0:T(8,128)(2,1)S(1)}, bf16[96,1024]{1,0:T(8,128)(2,1)S(1)}, u32[]{:S(2)}, u32[]{:S(2)}) %collective-permute-start.31) | collective-permute-done | bytes 196640 | tf_op jit(solution)/shard_map/gather_slope/ppermute | solution.py:57
  180.6 3.3 %collective-permute-start.33 = (bf16[48,1024]{1,0:T(8,128)(2,1)S(1)}, bf16[48,1024]{1,0:T(8,128)(2,1)S(1)}, u32[]{:S(2)}, u32[]{:S(2)}) collective-permute-start(bf16[48,1024]{1,0:T(8,128)(2,1)S(1)} %slice.202), channel_id=1, source_target_pairs={{0,3},{1,0},{2,1},{3,2},{4,7},{5,4},{6,5},{7,6},{8,11},{9,8},{10,9... | collective-permute-start | bytes 294920 | tf_op jit(solution)/shard_map/gather_slope/ppermute | solution.py:57
  188.4 3.2 %collective-permute-start.34 = (bf16[384,1024]{1,0:T(8,128)(2,1)S(1)}, bf16[384,1024]{1,0:T(8,128)(2,1)S(1)}, u32[]{:S(2)}, u32[]{:S(2)}) collective-permute-start(bf16[384,1024]{1,0:T(8,128)(2,1)S(1)} %get-tuple-element.62), channel_id=1, source_target_pairs={{0,12},{1,13},{2,14},{3,15},{4,0},{5,1},{6,2},{7,3},{8,4},{9,5},{1... | collective-permute-start | bytes 2359304 | tf_op jit(solution)/shard_map/gather_slope/ppermute | solution.py:57
  191.6 10.0 %collective-permute-done.35 = bf16[384,1024]{1,0:T(8,128)(2,1)S(1)} collective-permute-done((bf16[384,1024]{1,0:T(8,128)(2,1)S(1)}, bf16[384,1024]{1,0:T(8,128)(2,1)S(1)}, u32[]{:S(2)}, u32[]{:S(2)}) %collective-permute-start.35) | collective-permute-done | bytes 786464 | tf_op jit(solution)/shard_map/gather_slope/ppermute | solution.py:57
  201.7 3.3 %collective-permute-start.37 = (bf16[192,1024]{1,0:T(8,128)(2,1)S(1)}, bf16[192,1024]{1,0:T(8,128)(2,1)S(1)}, u32[]{:S(2)}, u32[]{:S(2)}) collective-permute-start(bf16[192,1024]{1,0:T(8,128)(2,1)S(1)} %slice.204), channel_id=1, source_target_pairs={{0,12},{1,13},{2,14},{3,15},{4,0},{5,1},{6,2},{7,3},{8,4},{9,5},{1... | collective-permute-start | bytes 1179656 | tf_op jit(solution)/shard_map/gather_slope/ppermute | solution.py:57
  205.0 11.9 %reshape.72 = bf16[1536,3,512]{2,1,0:T(4,128)(2,1)} reshape(bf16[16,96,1536]{2,1,0:T(8,128)(2,1)} %get-tuple-element.31) | data formatting | bytes 9437184 | tf_op jit(solution)/shard_map/step/reshape | solution.py:369
  220.4 10.3 %subtract_convert_fusion = bf16[3,512,1024]{2,1,0:T(8,128)(2,1)} fusion(f32[3,512,1024]{2,1,0:T(8,128)} %param.22, bf16[1536,1024]{1,0:T(8,128)(2,1)} %constant_dynamic-update-slice_fusion.10, bf16[1536,3,512]{2,1,0:T(4,128)(2,1)} %reshape.72), kind=kOutput, calls=%fused_computation | convolution fusion | flops 4836556800 | bytes 17301504 | tf_op jit(solution)/shard_map/step/zag,zh->agh/dot_general | solution.py:370
  (134 shorter events, 43.4 us)
Async XLA Ops:
  7.2 75.9 %all-gather.3.cloned.1.call-start = ((), (), s32[]{:S(2)}) async-start(), calls=%async_computation | async-start | bytes 4423680 | tf_op jit(solution)/shard_map/all_gather | solution.py:304
  30.8 11.3 %collective-permute-start.3 = (bf16[2,256,512]{2,1,0:T(8,128)(2,1)}, bf16[2,256,512]{2,1,0:T(8,128)(2,1)S(1)}, u32[]{:S(2)}, u32[]{:S(2)}) collective-permute-start(bf16[2,256,512]{2,1,0:T(8,128)(2,1)} %get-tuple-element.27), channel_id=1, source_target_pairs={{0,12},{1,13},{2,14},{3,15},{4,0},{5,1},{6,2},{7,3},{8,4},{9,5},{1... | collective-permute-start | bytes 1572872 | tf_op jit(solution)/shard_map/reduce_down/ppermute | solution.py:57
  35.1 11.9 %collective-permute-start = (bf16[2,256,512]{2,1,0:T(8,128)(2,1)}, bf16[2,256,512]{2,1,0:T(8,128)(2,1)S(1)}, u32[]{:S(2)}, u32[]{:S(2)}) collective-permute-start(bf16[2,256,512]{2,1,0:T(8,128)(2,1)} %get-tuple-element.23), channel_id=1, source_target_pairs={{0,4},{1,5},{2,6},{3,7},{4,8},{5,9},{6,10},{7,11},{8,12},{9,13},{1... | collective-permute-start | bytes 1572872 | tf_op jit(solution)/shard_map/reduce_down/ppermute | solution.py:57
  35.1 16.2 %collective-permute-start.5 = (bf16[2,256,512]{2,1,0:T(8,128)(2,1)}, bf16[2,256,512]{2,1,0:T(8,128)(2,1)S(1)}, u32[]{:S(2)}, u32[]{:S(2)}) collective-permute-start(bf16[2,256,512]{2,1,0:T(8,128)(2,1)} %get-tuple-element.28), channel_id=1, source_target_pairs={{0,4},{1,5},{2,6},{3,7},{4,8},{5,9},{6,10},{7,11},{8,12},{9,13},{1... | collective-permute-start | bytes 1572872 | tf_op jit(solution)/shard_map/reduce_down/ppermute | solution.py:57
  43.3 10.4 %collective-permute-start.4 = (bf16[2,256,512]{2,1,0:T(8,128)(2,1)S(1)}, bf16[2,256,512]{2,1,0:T(8,128)(2,1)S(1)}, u32[]{:S(2)}, u32[]{:S(2)}) collective-permute-start(bf16[2,256,512]{2,1,0:T(8,128)(2,1)S(1)} %add_convert_fusion), channel_id=1, source_target_pairs={{0,12},{1,13},{2,14},{3,15},{4,0},{5,1},{6,2},{7,3},{8,4},{9,5},{1... | collective-permute-start | bytes 1572872 | tf_op jit(solution)/shard_map/reduce_down/ppermute | solution.py:57
  46.9 13.8 %collective-permute-start.2 = (bf16[2,256,512]{2,1,0:T(8,128)(2,1)}, bf16[2,256,512]{2,1,0:T(8,128)(2,1)S(1)}, u32[]{:S(2)}, u32[]{:S(2)}) collective-permute-start(bf16[2,256,512]{2,1,0:T(8,128)(2,1)} %get-tuple-element.24), channel_id=1, source_target_pairs={{0,12},{1,13},{2,14},{3,15},{4,0},{5,1},{6,2},{7,3},{8,4},{9,5},{1... | collective-permute-start | bytes 1572872 | tf_op jit(solution)/shard_map/reduce_down/ppermute | solution.py:57
  48.2 12.6 %collective-permute-start.1 = (bf16[2,256,512]{2,1,0:T(8,128)(2,1)S(1)}, bf16[2,256,512]{2,1,0:T(8,128)(2,1)S(1)}, u32[]{:S(2)}, u32[]{:S(2)}) collective-permute-start(bf16[2,256,512]{2,1,0:T(8,128)(2,1)S(1)} %add_convert_fusion.1), channel_id=1, source_target_pairs={{0,4},{1,5},{2,6},{3,7},{4,8},{5,9},{6,10},{7,11},{8,12},{9,13},{1... | collective-permute-start | bytes 1572872 | tf_op jit(solution)/shard_map/reduce_down/ppermute | solution.py:57
  53.9 10.2 %collective-permute-start.6 = (bf16[128,512]{1,0:T(8,128)(2,1)S(1)}, bf16[128,512]{1,0:T(8,128)(2,1)S(1)}, u32[]{:S(2)}, u32[]{:S(2)}) collective-permute-start(bf16[128,512]{1,0:T(8,128)(2,1)S(1)} %get-tuple-element.52), channel_id=1, source_target_pairs={{0,1},{1,2},{2,3},{3,0},{4,5},{5,6},{6,7},{7,4},{8,9},{9,10},{10,1... | collective-permute-start | bytes 393224 | tf_op jit(solution)/shard_map/reduce_down/ppermute | solution.py:57
  61.1 8.2 %collective-permute-start.9 = (bf16[256,512]{1,0:T(8,128)(2,1)S(1)}, bf16[256,512]{1,0:T(8,128)(2,1)S(1)}, u32[]{:S(2)}, u32[]{:S(2)}) collective-permute-start(bf16[256,512]{1,0:T(8,128)(2,1)S(1)} %pad_maximum_fusion.3), channel_id=1, source_target_pairs={{0,3},{1,0},{2,1},{3,2},{4,7},{5,4},{6,5},{7,6},{8,11},{9,8},{10,9... | collective-permute-start | bytes 786440 | tf_op jit(solution)/shard_map/reduce_down/ppermute | solution.py:57
  64.2 7.7 %collective-permute-start.7 = (bf16[256,512]{1,0:T(8,128)(2,1)S(1)}, bf16[256,512]{1,0:T(8,128)(2,1)S(1)}, u32[]{:S(2)}, u32[]{:S(2)}) collective-permute-start(bf16[256,512]{1,0:T(8,128)(2,1)S(1)} %pad_maximum_fusion.2), channel_id=1, source_target_pairs={{0,1},{1,2},{2,3},{3,0},{4,5},{5,6},{6,7},{7,4},{8,9},{9,10},{10,1... | collective-permute-start | bytes 786440 | tf_op jit(solution)/shard_map/reduce_down/ppermute | solution.py:57
  72.2 6.3 %collective-permute-start.12 = (bf16[96,512]{1,0:T(8,128)(2,1)S(1)}, bf16[96,512]{1,0:T(8,128)(2,1)S(1)}, u32[]{:S(2)}, u32[]{:S(2)}) collective-permute-start(bf16[96,512]{1,0:T(8,128)(2,1)S(1)} %get-tuple-element.79), channel_id=1, source_target_pairs={{0,32},{1,33},{2,34},{3,35},{4,36},{5,37},{6,38},{7,39},{8,40},{9,... | collective-permute-start | bytes 294920 | tf_op jit(solution)/shard_map/late/ppermute | solution.py:57
  73.9 6.3 %collective-permute-start.11 = (bf16[96,512]{1,0:T(8,128)(2,1)S(1)}, bf16[96,512]{1,0:T(8,128)(2,1)S(1)}, u32[]{:S(2)}, u32[]{:S(2)}) collective-permute-start(bf16[96,512]{1,0:T(8,128)(2,1)S(1)} %get-tuple-element.79), channel_id=1, source_target_pairs={{0,64},{1,65},{2,66},{3,67},{4,68},{5,69},{6,70},{7,71},{8,72},{9,... | collective-permute-start | bytes 294920 | tf_op jit(solution)/shard_map/late/ppermute | solution.py:57
  116.9 9.3 %collective-permute-start.17 = (bf16[2,96,1024]{2,1,0:T(8,128)(2,1)}, bf16[2,96,1024]{2,1,0:T(8,128)(2,1)S(1)}, u32[]{:S(2)}, u32[]{:S(2)}) collective-permute-start(bf16[2,96,1024]{2,1,0:T(8,128)(2,1)} %get-tuple-element.38), channel_id=1, source_target_pairs={{0,12},{1,13},{2,14},{3,15},{4,0},{5,1},{6,2},{7,3},{8,4},{9,5},{1... | collective-permute-start | bytes 1179656 | tf_op jit(solution)/shard_map/reduce_draft/ppermute | solution.py:57
  120.8 11.0 %collective-permute-start.14 = (bf16[2,96,1024]{2,1,0:T(8,128)(2,1)}, bf16[2,96,1024]{2,1,0:T(8,128)(2,1)S(1)}, u32[]{:S(2)}, u32[]{:S(2)}) collective-permute-start(bf16[2,96,1024]{2,1,0:T(8,128)(2,1)} %get-tuple-element.34), channel_id=1, source_target_pairs={{0,4},{1,5},{2,6},{3,7},{4,8},{5,9},{6,10},{7,11},{8,12},{9,13},{1... | collective-permute-start | bytes 1179656 | tf_op jit(solution)/shard_map/reduce_draft/ppermute | solution.py:57
  120.9 18.9 %collective-permute-start.19 = (bf16[2,96,1024]{2,1,0:T(8,128)(2,1)}, bf16[2,96,1024]{2,1,0:T(8,128)(2,1)S(1)}, u32[]{:S(2)}, u32[]{:S(2)}) collective-permute-start(bf16[2,96,1024]{2,1,0:T(8,128)(2,1)} %get-tuple-element.39), channel_id=1, source_target_pairs={{0,4},{1,5},{2,6},{3,7},{4,8},{5,9},{6,10},{7,11},{8,12},{9,13},{1... | collective-permute-start | bytes 1179656 | tf_op jit(solution)/shard_map/reduce_draft/ppermute | solution.py:57
  127.3 12.5 %collective-permute-start.18 = (bf16[2,96,1024]{2,1,0:T(8,128)(2,1)S(1)}, bf16[2,96,1024]{2,1,0:T(8,128)(2,1)S(1)}, u32[]{:S(2)}, u32[]{:S(2)}) collective-permute-start(bf16[2,96,1024]{2,1,0:T(8,128)(2,1)S(1)} %add_convert_fusion.2), channel_id=1, source_target_pairs={{0,12},{1,13},{2,14},{3,15},{4,0},{5,1},{6,2},{7,3},{8,4},{9,5},{1... | collective-permute-start | bytes 1179656 | tf_op jit(solution)/shard_map/reduce_draft/ppermute | solution.py:57
  131.0 24.1 %collective-permute-start.24 = (bf16[96,512]{1,0:T(8,128)(2,1)S(1)}, bf16[96,512]{1,0:T(8,128)(2,1)S(1)}, u32[]{:S(2)}, u32[]{:S(2)}) collective-permute-start(bf16[96,512]{1,0:T(8,128)(2,1)S(1)} %get-tuple-element.68), channel_id=1, source_target_pairs={{0,0},{1,1},{2,16},{3,17},{4,32},{5,33},{6,48},{7,49},{8,64},{9,65... | collective-permute-start | bytes 294920 | tf_op jit(solution)/shard_map/targets/ppermute | solution.py:57
  131.7 23.4 %collective-permute-start.25 = (bf16[96,512]{1,0:T(8,128)(2,1)S(1)}, bf16[96,512]{1,0:T(8,128)(2,1)S(1)}, u32[]{:S(2)}, u32[]{:S(2)}) collective-permute-start(bf16[96,512]{1,0:T(8,128)(2,1)S(1)} %get-tuple-element.69), channel_id=1, source_target_pairs={{0,1},{1,0},{2,17},{3,16},{4,33},{5,32},{6,49},{7,48},{8,65},{9,64... | collective-permute-start | bytes 294920 | tf_op jit(solution)/shard_map/targets/ppermute | solution.py:57
  131.8 15.7 %collective-permute-start.16 = (bf16[2,96,1024]{2,1,0:T(8,128)(2,1)}, bf16[2,96,1024]{2,1,0:T(8,128)(2,1)S(1)}, u32[]{:S(2)}, u32[]{:S(2)}) collective-permute-start(bf16[2,96,1024]{2,1,0:T(8,128)(2,1)} %get-tuple-element.35), channel_id=1, source_target_pairs={{0,12},{1,13},{2,14},{3,15},{4,0},{5,1},{6,2},{7,3},{8,4},{9,5},{1... | collective-permute-start | bytes 1179656 | tf_op jit(solution)/shard_map/reduce_draft/ppermute | solution.py:57
  139.8 9.1 %collective-permute-start.15 = (bf16[2,96,1024]{2,1,0:T(8,128)(2,1)S(1)}, bf16[2,96,1024]{2,1,0:T(8,128)(2,1)S(1)}, u32[]{:S(2)}, u32[]{:S(2)}) collective-permute-start(bf16[2,96,1024]{2,1,0:T(8,128)(2,1)S(1)} %add_convert_fusion.3), channel_id=1, source_target_pairs={{0,4},{1,5},{2,6},{3,7},{4,8},{5,9},{6,10},{7,11},{8,12},{9,13},{1... | collective-permute-start | bytes 1179656 | tf_op jit(solution)/shard_map/reduce_draft/ppermute | solution.py:57
  140.1 10.2 %collective-permute-start.22 = (bf16[48,1024]{1,0:T(8,128)(2,1)S(1)}, bf16[48,1024]{1,0:T(8,128)(2,1)S(1)}, u32[]{:S(2)}, u32[]{:S(2)}) collective-permute-start(bf16[48,1024]{1,0:T(8,128)(2,1)S(1)} %get-tuple-element.56), channel_id=1, source_target_pairs={{0,3},{1,0},{2,1},{3,2},{4,7},{5,4},{6,5},{7,6},{8,11},{9,8},{10,9... | collective-permute-start | bytes 294920 | tf_op jit(solution)/shard_map/reduce_draft/ppermute | solution.py:57
  149.0 5.9 %collective-permute-start.20 = (bf16[48,1024]{1,0:T(8,128)(2,1)S(1)}, bf16[48,1024]{1,0:T(8,128)(2,1)S(1)}, u32[]{:S(2)}, u32[]{:S(2)}) collective-permute-start(bf16[48,1024]{1,0:T(8,128)(2,1)S(1)} %get-tuple-element.55), channel_id=1, source_target_pairs={{0,1},{1,2},{2,3},{3,0},{4,5},{5,6},{6,7},{7,4},{8,9},{9,10},{10,1... | collective-permute-start | bytes 294920 | tf_op jit(solution)/shard_map/reduce_draft/ppermute | solution.py:57
  155.0 6.9 %collective-permute-start.21 = (bf16[96,1024]{1,0:T(8,128)(2,1)S(1)}, bf16[96,1024]{1,0:T(8,128)(2,1)S(1)}, u32[]{:S(2)}, u32[]{:S(2)}) collective-permute-start(bf16[96,1024]{1,0:T(8,128)(2,1)S(1)} %pad_maximum_fusion.4), channel_id=1, source_target_pairs={{0,1},{1,2},{2,3},{3,0},{4,5},{5,6},{6,7},{7,4},{8,9},{9,10},{10,1... | collective-permute-start | bytes 589832 | tf_op jit(solution)/shard_map/reduce_draft/ppermute | solution.py:57
  163.4 6.4 %collective-permute-start.28 = (f32[3,96]{1,0:T(4,128)S(1)}, f32[3,96]{1,0:T(4,128)S(1)}, u32[]{:S(2)}, u32[]{:S(2)}) collective-permute-start(f32[3,96]{1,0:T(4,128)S(1)} %fusion.55), channel_id=1, source_target_pairs={{0,64},{1,65},{2,66},{3,67},{4,68},{5,69},{6,70},{7,71},{8,72},{9,... | collective-permute-start | bytes 3464 | tf_op jit(solution)/shard_map/norm/ppermute | solution.py:57
  173.5 6.9 %collective-permute-start.31 = (bf16[96,1024]{1,0:T(8,128)(2,1)S(1)}, bf16[96,1024]{1,0:T(8,128)(2,1)S(1)}, u32[]{:S(2)}, u32[]{:S(2)}) collective-permute-start(bf16[96,1024]{1,0:T(8,128)(2,1)S(1)} %get-tuple-element.44), channel_id=1, source_target_pairs={{0,1},{1,2},{2,3},{3,0},{4,5},{5,6},{6,7},{7,4},{8,9},{9,10},{10,1... | collective-permute-start | bytes 589832 | tf_op jit(solution)/shard_map/gather_slope/ppermute | solution.py:57
  173.6 7.0 %collective-permute-start.30 = (bf16[96,1024]{1,0:T(8,128)(2,1)S(1)}, bf16[96,1024]{1,0:T(8,128)(2,1)S(1)}, u32[]{:S(2)}, u32[]{:S(2)}) collective-permute-start(bf16[96,1024]{1,0:T(8,128)(2,1)S(1)} %get-tuple-element.44), channel_id=1, source_target_pairs={{0,3},{1,0},{2,1},{3,2},{4,7},{5,4},{6,5},{7,6},{8,11},{9,8},{10,9... | collective-permute-start | bytes 589832 | tf_op jit(solution)/shard_map/gather_slope/ppermute | solution.py:57
  180.5 5.9 %collective-permute-start.32 = (bf16[48,1024]{1,0:T(8,128)(2,1)S(1)}, bf16[48,1024]{1,0:T(8,128)(2,1)S(1)}, u32[]{:S(2)}, u32[]{:S(2)}) collective-permute-start(bf16[48,1024]{1,0:T(8,128)(2,1)S(1)} %slice.201), channel_id=1, source_target_pairs={{0,1},{1,2},{2,3},{3,0},{4,5},{5,6},{6,7},{7,4},{8,9},{9,10},{10,1... | collective-permute-start | bytes 294920 | tf_op jit(solution)/shard_map/gather_slope/ppermute | solution.py:57
  180.6 6.4 %collective-permute-start.33 = (bf16[48,1024]{1,0:T(8,128)(2,1)S(1)}, bf16[48,1024]{1,0:T(8,128)(2,1)S(1)}, u32[]{:S(2)}, u32[]{:S(2)}) collective-permute-start(bf16[48,1024]{1,0:T(8,128)(2,1)S(1)} %slice.202), channel_id=1, source_target_pairs={{0,3},{1,0},{2,1},{3,2},{4,7},{5,4},{6,5},{7,6},{8,11},{9,8},{10,9... | collective-permute-start | bytes 294920 | tf_op jit(solution)/shard_map/gather_slope/ppermute | solution.py:57
  188.4 13.2 %collective-permute-start.35 = (bf16[384,1024]{1,0:T(8,128)(2,1)S(1)}, bf16[384,1024]{1,0:T(8,128)(2,1)S(1)}, u32[]{:S(2)}, u32[]{:S(2)}) collective-permute-start(bf16[384,1024]{1,0:T(8,128)(2,1)S(1)} %get-tuple-element.62), channel_id=1, source_target_pairs={{0,4},{1,5},{2,6},{3,7},{4,8},{5,9},{6,10},{7,11},{8,12},{9,13},{1... | collective-permute-start | bytes 2359304 | tf_op jit(solution)/shard_map/gather_slope/ppermute | solution.py:57
  188.4 13.3 %collective-permute-start.34 = (bf16[384,1024]{1,0:T(8,128)(2,1)S(1)}, bf16[384,1024]{1,0:T(8,128)(2,1)S(1)}, u32[]{:S(2)}, u32[]{:S(2)}) collective-permute-start(bf16[384,1024]{1,0:T(8,128)(2,1)S(1)} %get-tuple-element.62), channel_id=1, source_target_pairs={{0,12},{1,13},{2,14},{3,15},{4,0},{5,1},{6,2},{7,3},{8,4},{9,5},{1... | collective-permute-start | bytes 2359304 | tf_op jit(solution)/shard_map/gather_slope/ppermute | solution.py:57
  201.6 16.3 %collective-permute-start.36 = (bf16[192,1024]{1,0:T(8,128)(2,1)S(1)}, bf16[192,1024]{1,0:T(8,128)(2,1)S(1)}, u32[]{:S(2)}, u32[]{:S(2)}) collective-permute-start(bf16[192,1024]{1,0:T(8,128)(2,1)S(1)} %slice.203), channel_id=1, source_target_pairs={{0,4},{1,5},{2,6},{3,7},{4,8},{5,9},{6,10},{7,11},{8,12},{9,13},{1... | collective-permute-start | bytes 1179656 | tf_op jit(solution)/shard_map/gather_slope/ppermute | solution.py:57
  201.7 16.9 %collective-permute-start.37 = (bf16[192,1024]{1,0:T(8,128)(2,1)S(1)}, bf16[192,1024]{1,0:T(8,128)(2,1)S(1)}, u32[]{:S(2)}, u32[]{:S(2)}) collective-permute-start(bf16[192,1024]{1,0:T(8,128)(2,1)S(1)} %slice.204), channel_id=1, source_target_pairs={{0,12},{1,13},{2,14},{3,15},{4,0},{5,1},{6,2},{7,3},{8,4},{9,5},{1... | collective-permute-start | bytes 1179656 | tf_op jit(solution)/shard_map/gather_slope/ppermute | solution.py:57
  (16 other events, 199.9 us)
Sparse Core Ops, SparseCore 0:
  12.2 33.5 all-gather.2

commit v2 on v1

v2 whole, which is shorter than its diff:
```python
import functools

import jax
import jax.numpy as jnp
from jax import lax
from jax.experimental import pallas as pl
from jax.experimental.pallas import tpu as pltpu
from jax.sharding import PartitionSpec as P

step_rate = 8.0
epsilon = 1e-06
side = 4
cores = 2
block_units = 32
f32 = jnp.float32
bf16 = jnp.bfloat16
mesh_axes = ("replica", "tensor")
vmem = 56 * 1024 * 1024


def coordinates(device):
    replica, tensor = divmod(device, side * side)
    x, c = divmod(replica, cores)
    z, y = divmod(tensor, side)
    return x, c, z, y


def device_at(x, c, z, y):
    return ((x % side) * cores + c % cores) * side * side + (z % side) * side + y % side


def moved(target):
    return [(d, target(*coordinates(d))) for d in range(side * cores * side * side)]


def along_first(shift):
    return moved(
        lambda x, c, z, y: device_at(x, c, z + shift * (c == 0), y + shift * (c == 1))
    )


def along_second(shift):
    return moved(
        lambda x, c, z, y: device_at(x, c, z + shift * (c == 1), y + shift * (c == 0))
    )


def along_x(shift):
    return moved(lambda x, c, z, y: device_at(x + shift, c, z, y))


def other_core():
    return moved(lambda x, c, z, y: device_at(x, 1 - c, z, y))


def send(array, pairs):
    return lax.ppermute(array, mesh_axes, pairs)


def plus(*terms):
    return functools.reduce(jnp.add, [term.astype(f32) for term in terms])


def other_core_rows():
    return moved(lambda x, c, z, y: device_at(x, 1 - c, y, z))


def row_block(c, tensor):
    z, y = tensor // side, tensor % side
    return z * side + y if c == 0 else y * side + z


def turned(pieces, places):
    for bit in (1, 2):
        moves = places // bit % 2 == 1
        pieces = [
            jnp.where(moves, pieces[(j - bit) % side], pieces[j]) for j in range(side)
        ]
    return pieces


def place():
    replica, tensor = lax.axis_index("replica"), lax.axis_index("tensor")
    x, c = replica // cores, replica % cores
    z, y = tensor // side, tensor % side
    return x, c, jnp.where(c == 0, z, y), jnp.where(c == 0, y, z)


def down_kernel(block_ref, tokens_ref, coded_ref, exponent_ref, *pieces):
    i = pl.program_id(0)
    units, columns = coded_ref.shape
    factor = jnp.exp2(exponent_ref[...].astype(f32) - 127.0).astype(bf16)
    weight = coded_ref[...].reshape(units // block_units, block_units, columns)
    weight = (weight * factor[:, None, :]).reshape(units, columns)
    total = jnp.dot(tokens_ref[...], weight, preferred_element_type=f32)
    for k in range(len(pieces)):

        @pl.when(i // 2 == k)
        def _():
            pieces[k][0] = total.astype(pieces[k].dtype)


def down_pieces(blocks, tokens, coded_weight, block_exponent, kind):
    rows, units = tokens.shape
    width = coded_weight.shape[1] // (side * side)
    count = blocks.shape[0]

    def piece(k):
        return pl.BlockSpec(
            (1, rows, width), lambda i, blocks: (jnp.clip(i - 2 * k, 0, 1), 0, 0)
        )

    return pl.pallas_call(
        down_kernel,
        grid_spec=pltpu.PrefetchScalarGridSpec(
            num_scalar_prefetch=1,
            grid=(count,),
            in_specs=[
                pl.BlockSpec((rows, units), lambda i, blocks: (0, 0)),
                pl.BlockSpec((units, width), lambda i, blocks: (0, blocks[i])),
                pl.BlockSpec((units // block_units, width), lambda i, blocks: (0, blocks[i])),
            ],
            out_specs=[piece(k) for k in range(count // 2)],
        ),
        out_shape=[jax.ShapeDtypeStruct((2, rows, width), kind)] * (count // 2),
        compiler_params=pltpu.CompilerParams(vmem_limit_bytes=vmem),
        cost_estimate=pl.CostEstimate(
            flops=2 * rows * units * width * count,
            bytes_accessed=3 * units * width * count,
            transcendentals=0,
        ),
        name="down_projection",
    )(blocks, tokens, coded_weight, block_exponent)


def reduce_blocks(near, direct, own, q):
    low_right = send(near[0], along_first(1))
    high_left = send(near[1], along_first(-1))
    high_right = send(direct[1], along_first(1))
    low_left = send(direct[2], along_first(-1))
    low_right = send(plus(direct[0], low_right).astype(bf16), along_first(1))
    high_left = send(plus(direct[3], high_left).astype(bf16), along_first(-1))
    summed = jnp.concatenate(
        [plus(own[0], low_right, low_left), plus(own[1], high_left, high_right)]
    )
    halved = summed.astype(bf16)

    def at(array, shift):
        return lax.dynamic_index_in_dim(array, (q + shift) % side, 0, keepdims=False)

    parts = [send(at(halved, shift), along_second(shift)) for shift in (1, 3, 2)]
    return plus(at(summed, 0), *parts)


def body(
    gated_hidden,
    coded_weight,
    block_exponent,
    stream_input,
    lower_layer,
    middle_layer,
    prior_lower,
    prior_middle,
    prior_upper,
    accepted,
    draft_input_weight,
    draft_gain,
):
    steps, rows, unit_count = gated_hidden.shape
    feature_slice = stream_input.shape[2]
    out_slice = draft_input_weight.shape[2]
    replicas = lax.axis_size("replica")
    tensors = lax.axis_size("tensor")
    width = feature_slice * tensors
    slots_all = steps * rows * replicas
    slots = rows * 3 // 4
    x, c, p, q = place()

    with jax.named_scope("down"):
        tokens = gated_hidden.reshape(steps * rows, unit_count)
        second = jnp.arange(side, dtype=jnp.int32)

        def columns(shift):
            first = (p + shift) % side
            return jnp.where(c == 0, first * side + second, second * side + first)

        near = down_pieces(columns(2), tokens, coded_weight, block_exponent, bf16)
        near, accepted = lax.optimization_barrier((near, accepted))

    with jax.named_scope("select"):
        row = jnp.arange(rows, dtype=jnp.int32)
        before = row[:, None] <= row[None, :]
        first_live = (accepted >= 1).astype(jnp.int32)
        second_live = (accepted >= 2).astype(jnp.int32)
        first_slot = jnp.sum(jnp.where(before, first_live[:, None], 0), axis=0) - 1
        second_slot = 2 * slots - jnp.sum(jnp.where(before, second_live[:, None], 0), axis=0)
        first_slot = jnp.where(first_live == 1, first_slot, -1)
        second_slot = jnp.where(second_live == 1, second_slot, -1)
        slot = jnp.arange(2 * slots, dtype=jnp.int32)[:, None]
        select = (slot == jnp.concatenate([first_slot, second_slot])[None, :]).astype(bf16)

        def pick(chosen, first, second):
            return jnp.dot(
                chosen, jnp.concatenate([first, second]), preferred_element_type=f32
            ).astype(bf16)

        pair = pick(
            select,
            jnp.concatenate([prior_lower, prior_middle], axis=1),
            jnp.concatenate([lower_layer, middle_layer], axis=1),
        )
        front = jnp.dot(
            select[:slots, :rows], prior_upper, preferred_element_type=f32
        ).astype(bf16)
        folded = jnp.concatenate([front[: slots // 2], front[slots // 2 :]], axis=1)
        payload = jnp.concatenate([pair, folded])
    gathered = lax.all_gather(payload, "replica", axis=0, tiled=True)

    with jax.named_scope("down"):
        others, payload = lax.optimization_barrier(
            (jnp.concatenate([columns(1), columns(3)]), payload)
        )
        direct = down_pieces(others, tokens, coded_weight, block_exponent, bf16)
        direct, draft_weight = lax.optimization_barrier((direct, draft_input_weight))
        rounded = draft_weight.astype(bf16)
        mine, rounded = lax.optimization_barrier((columns(0), rounded))
        own = down_pieces(mine, tokens, coded_weight, block_exponent, f32)

    with jax.named_scope("reduce_down"):
        summed = reduce_blocks(near, direct, own, q)
    upper_layer = (
        stream_input.astype(f32) + summed.reshape(steps, rows, feature_slice)
    ).astype(bf16)

    with jax.named_scope("back"):
        back = pick(select[slots:], prior_upper, upper_layer[0])
        chips = [back] + [send(back, along_x(-shift)) for shift in (1, 2, 3)]
        chips = jnp.stack(turned(chips, x))
        others = send(chips, other_core())
        backs = jnp.stack(
            [jnp.where(c == 0, chips, others), jnp.where(c == 0, others, chips)], axis=1
        ).reshape(replicas, slots, feature_slice)

    with jax.named_scope("targets"):
        chosen = pick(select, upper_layer[0], upper_layer[1])
        parity = lax.axis_index("tensor") % 2
        even, odd = chosen[:slots], chosen[slots:]
        got = []
        for turn in range(2):
            routes = []
            for d in range(replicas * tensors):
                r, t = divmod(d, tensors)
                owner = t // 2
                taken = row_block(owner % cores, 2 * r + (t + turn) % 2)
                routes.append((d, owner * tensors + taken))
            got.append(send(jnp.where((parity + turn) % 2 == 0, even, odd), routes))

    with jax.named_scope("early"):
        gathered, upper_layer = lax.optimization_barrier((gathered, upper_layer))
        early = jnp.dot(
            gathered,
            rounded[:2].reshape(2 * feature_slice, out_slice),
            preferred_element_type=f32,
        )
        gathered = gathered.reshape(replicas, -1, 2 * feature_slice)
        stride = gathered.shape[1]
        pairs, fronts = gathered[:, : 2 * slots], gathered[:, 2 * slots :]
        fronts = jnp.concatenate(
            [fronts[:, :, :feature_slice], fronts[:, :, feature_slice:]], axis=1
        )

    with jax.named_scope("late"):
        backs, got, early = lax.optimization_barrier((backs, got, early))
        thirds = jnp.concatenate([fronts, backs], axis=1).reshape(-1, feature_slice)

        def drafted_piece(third_weight, shift, half, kind):
            replica = 2 * ((p + shift) % side) + half
            total = lax.dynamic_slice_in_dim(early, replica * stride, 2 * slots, axis=0) + jnp.dot(
                lax.dynamic_slice_in_dim(thirds, replica * 2 * slots, 2 * slots, axis=0),
                third_weight,
                preferred_element_type=f32,
            )
            return total.astype(kind).reshape(2, slots, out_slice)

        third_weight = rounded[2]
        near = [drafted_piece(third_weight, 2, half, bf16) for half in range(2)]
        near, third_weight = lax.optimization_barrier((near, third_weight))
        direct = [
            drafted_piece(third_weight, shift, half, bf16) for shift in (1, 3) for half in range(2)
        ]
        direct, third_weight = lax.optimization_barrier((direct, third_weight))
        own = [drafted_piece(third_weight, 0, half, f32) for half in range(2)]

    with jax.named_scope("reduce_draft"):
        drafted = reduce_blocks(near, direct, own, q)

    with jax.named_scope("norm"):
        front_rows = q % 2 == 0
        targets = jnp.concatenate(
            [jnp.where(front_rows, got[0], got[1]), jnp.where(front_rows, got[1], got[0])],
            axis=1,
        ).astype(f32)
        gain = draft_gain[None, :]
        scaled = gain * drafted
        sums = jnp.stack(
            [
                jnp.sum(drafted * drafted, axis=1),
                jnp.sum(scaled * scaled, axis=1),
                jnp.sum(scaled * targets, axis=1),
            ]
        )
        sums = sums + send(sums, other_core_rows())
        sums = sums + send(sums, along_x(1)) + send(sums, along_x(2)) + send(sums, along_x(3))
        scale = lax.rsqrt(sums[0] / width + epsilon)
        inner = (scale * sums[1] - sums[2]) / slots_all
        error = gain * (scaled * scale[:, None] - targets) / slots_all
        slope = (scale[:, None] * error - drafted * (scale**3 * inner / width)[:, None]).astype(
            bf16
        )

    with jax.named_scope("gather_slope"):
        ring = [slope] + [send(slope, along_second(-shift)) for shift in (1, 2, 3)]
        ring = jnp.concatenate(turned(ring, q))
        previous = send(ring, along_first(1))
        following = send(ring, along_first(-1))
        previous, following, low, high = lax.optimization_barrier(
            (previous, following, previous[: 2 * slots], following[2 * slots :])
        )
        low = send(low, along_first(1))
        high = send(high, along_first(-1))

    with jax.named_scope("step"):
        features = jnp.concatenate([pairs.reshape(-1, 2 * feature_slice), thirds], axis=1)

        def product(shift, slopes):
            start = (p + shift) % side * side * slots
            inputs = lax.dynamic_slice_in_dim(features, start, side * slots, axis=0)
            return lax.dot_general(
                inputs, slopes, (((0,), (0,)), ((), ())), preferred_element_type=f32
            )

        total = lax.optimization_barrier(product(0, ring))
        total = lax.optimization_barrier(total + product(1, following))
        total = lax.optimization_barrier(total + product(3, previous))
        total = total + product(2, jnp.concatenate([low, high]))
        new_weight = (draft_input_weight.reshape(total.shape) - step_rate * total).astype(bf16)
        new_weight = new_weight.reshape(draft_input_weight.shape)
    return (upper_layer, new_weight)


def solution(mesh):
    return jax.shard_map(
        body,
        mesh=mesh,
        in_specs=(
            P(None, "replica", "tensor"),
            P("tensor", None),
            P("tensor", None),
            P(None, "replica", "tensor"),
            P("replica", "tensor"),
            P("replica", "tensor"),
            P("replica", "tensor"),
            P("replica", "tensor"),
            P("replica", "tensor"),
            P("replica"),
            P(None, "tensor", "replica"),
            P("replica"),
        ),
        out_specs=(P(None, "replica", "tensor"), P(None, "tensor", "replica")),
        check_vma=False,
    )
```

time: 239 us -> 195 us (0.82)
  Pallas kernels: 52 us -> 21.7 us
  waiting for transfers between devices: 61.5 us -> 49.1 us
  local copies, waits for them, and re-layouts: 19.1 us -> 6.73 us
  matrix products: 13.1 us -> 20.1 us
  starting transfers between devices: 62.5 us -> 66 us
    pallas_call x2 -> x0, Pallas kernels: 33.8 us -> none  [the longest x1 18.8 us: early_projection(): pl.pallas_call(early_kernel, grid_spec=pltpu.PrefetchScalarGridSpec(num_s...]
    ppermute x38 -> x35, waiting for transfers between devices: 61.4 us -> 49 us  [send(): return lax.ppermute(array, mesh_axes, pairs)]
    reshape x1 -> x0, local copies, waits for them, and re-layouts: 11.9 us -> none  [body(): inputs = features.reshape(-1, 3, feature_slice)]
    dot_general x1 -> x13, matrix products: 10.3 us -> 19.3 us  [the longest x4 9.69 us: product(): lax.dot_general(inputs, slopes, (((0,), (0,)), ((), ())), preferred_eleme...]
    unnamed x28 -> x36, local copies, waits for them, and re-layouts: 5.33 us -> 1.2 us
    pallas_call x1 -> x3, Pallas kernels: 18.1 us -> 21.7 us  [down_pieces(): pl.pallas_call(down_kernel, grid_spec=pltpu.PrefetchScalarGridSpec(num_sc...]
    slice x7, local copies, waits for them, and re-layouts: 0.13 us -> 3.67 us  [the longest x1 2.27 us: body(): pairs, fronts = (gathered[:, :2 * slots], gathered[:, 2 * slots:])]
    ppermute x38 -> x35, starting transfers between devices: 62.5 us -> 65.9 us  [send(): return lax.ppermute(array, mesh_axes, pairs)]
  transfers between devices with their start and end apart: 39 -> 36, of which waited for: 20 -> 21; matrix products, arithmetic and copies ran while one was open for 12% -> 15% of each run, Pallas kernels for 8% -> 8%
where the time goes in v2:
time: 195 us; the launch traced here: 194 us
  starting transfers between devices  66 us (34%)
  waiting for transfers between devices  49.1 us (25%)
  Pallas kernels  21.7 us (11%)
  matrix products  20.1 us (10%)
  between operations  15 us (8%)
  other arithmetic  14.9 us (8%)
  local copies, waits for them, and re-layouts  6.73 us (3%)
    ppermute x35, starting transfers between devices, send(): return lax.ppermute(array, mesh_axes, pairs)  65.9 us
    ppermute x35, waiting for transfers between devices, send(): return lax.ppermute(array, mesh_axes, pairs)  49 us
    pallas_call x3, Pallas kernels, down_pieces(): pl.pallas_call(down_kernel, grid_spec=pltpu.PrefetchScalarGridSpec(num_sc...  21.7 us
    dot_general x4, matrix products, product(): lax.dot_general(inputs, slopes, (((0,), (0,)), ((), ())), preferred_eleme...  9.69 us
    dot_general x1, matrix products, body(): jnp.dot(gathered, rounded[:2].reshape(2 * feature_slice, out_slice), pref...  6.54 us
    convert_element_type x1, other arithmetic, body(): rounded = draft_weight.astype(bf16)  5.05 us
  transfers between devices with their start and end apart: 36, of which 21 were waited for; matrix products, arithmetic and copies ran while one was open for 15% of the time, Pallas kernels for 8%

profile of v2, /device:TPU:0, one launch (start us, length us, event | category | flops | bytes accessed | tf_op | source)
XLA Modules:
  0.0 193.6 jit_solution(1509525984480054642)
XLA Ops:
  7.8 5.9 %down_projection.3 = (bf16[2,256,512]{2,1,0:T(8,128)(2,1)}, bf16[2,256,512]{2,1,0:T(8,128)(2,1)}) custom-call(s32[4]{0:T(128)} %broadcast_select_fusion.19.block_ref, bf16[256,896]{1,0:T(8,128)(2,1)} %bitcast.119, bf16[896,8192]{1,0:T(8,128)(2,1)} %coded_ref.5, s32[28,8192]{1,0:T(8,128)} %exponent_ref.5), custom_call_target="tpu_custom_call" | custom-call | flops 939524096 | bytes 5505024 | tf_op jit(solution)/shard_map/down/down_projection/pallas_call | solution.py:113
  15.7 4.2 %collective-permute-start.3 = (bf16[2,256,512]{2,1,0:T(8,128)(2,1)S(1)}, bf16[2,256,512]{2,1,0:T(8,128)(2,1)S(1)}, u32[]{:S(2)}, u32[]{:S(2)}) collective-permute-start(bf16[2,256,512]{2,1,0:T(8,128)(2,1)S(1)} %copy-done.11), channel_id=1, source_target_pairs={{0,12},{1,13},{2,14},{3,15},{4,0},{5,1},{6,2},{7,3},{8,4},{9,5},{1... | collective-permute-start | bytes 1572872 | tf_op jit(solution)/shard_map/reduce_down/ppermute | solution.py:57
  20.5 9.7 %down_projection.4 = (bf16[2,256,512]{2,1,0:T(8,128)(2,1)}, bf16[2,256,512]{2,1,0:T(8,128)(2,1)}, bf16[2,256,512]{2,1,0:T(8,128)(2,1)}, bf16[2,256,512]{2,1,0:T(8,128)(2,1)}) custom-call(s32[8]{0:T(128)} %pad_add_fusion.1.block_ref, bf16[256,896]{1,0:T(8,128)(2,1)} %bitcast.120, bf16[896,8192]{1,0:T(8,128)(2,1)} %coded_ref.5, s32[28,8192]{1,0:T(8,128)} %exponent_ref.5), custom_call_target="tpu_custom_call" | custom-call | flops 1879048192 | bytes 11010048 | tf_op jit(solution)/shard_map/down/down_projection/pallas_call | solution.py:113
  31.5 3.3 %collective-permute-start.4 = (bf16[2,256,512]{2,1,0:T(8,128)(2,1)S(1)}, bf16[2,256,512]{2,1,0:T(8,128)(2,1)S(1)}, u32[]{:S(2)}, u32[]{:S(2)}) collective-permute-start(bf16[2,256,512]{2,1,0:T(8,128)(2,1)S(1)} %add_convert_fusion), channel_id=1, source_target_pairs={{0,12},{1,13},{2,14},{3,15},{4,0},{5,1},{6,2},{7,3},{8,4},{9,5},{1... | collective-permute-start | bytes 1572872 | tf_op jit(solution)/shard_map/reduce_down/ppermute | solution.py:57
  34.7 2.0 %collective-permute-start.2 = (bf16[2,256,512]{2,1,0:T(8,128)(2,1)}, bf16[2,256,512]{2,1,0:T(8,128)(2,1)S(1)}, u32[]{:S(2)}, u32[]{:S(2)}) collective-permute-start(bf16[2,256,512]{2,1,0:T(8,128)(2,1)} %get-tuple-element.52), channel_id=1, source_target_pairs={{0,12},{1,13},{2,14},{3,15},{4,0},{5,1},{6,2},{7,3},{8,4},{9,5},{1... | collective-permute-start | bytes 1572872 | tf_op jit(solution)/shard_map/reduce_down/ppermute | solution.py:57
  38.1 5.1 %convert_element_type.144 = bf16[3,512,1024]{2,1,0:T(8,128)(2,1)} convert(f32[3,512,1024]{2,1,0:T(8,128)} %param.22) | non-fusion elementwise | flops 1572864 | bytes 9437184 | tf_op jit(solution)/shard_map/down/convert_element_type | solution.py:225
  43.7 6.1 %down_projection.5 = (f32[2,256,512]{2,1,0:T(8,128)}, f32[2,256,512]{2,1,0:T(8,128)}) custom-call(s32[4]{0:T(128)} %broadcast_select_fusion.18.block_ref, bf16[256,896]{1,0:T(8,128)(2,1)} %bitcast.121, bf16[896,8192]{1,0:T(8,128)(2,1)} %coded_ref.5, s32[28,8192]{1,0:T(8,128)} %exponent_ref.5), custom_call_target="tpu_custom_call" | custom-call | flops 939524096 | bytes 5505024 | tf_op jit(solution)/shard_map/down/down_projection/pallas_call | solution.py:113
  58.7 2.6 %collective-permute-done.6 = bf16[256,512]{1,0:T(8,128)(2,1)S(1)} collective-permute-done((bf16[256,512]{1,0:T(8,128)(2,1)}, bf16[256,512]{1,0:T(8,128)(2,1)S(1)}, u32[]{:S(2)}, u32[]{:S(2)}) %collective-permute-start.6) | collective-permute-done | bytes 262176 | tf_op jit(solution)/shard_map/reduce_down/ppermute | solution.py:57
  61.5 3.8 %collective-permute-done.8 = bf16[256,512]{1,0:T(8,128)(2,1)S(1)} collective-permute-done((bf16[256,512]{1,0:T(8,128)(2,1)S(1)}, bf16[256,512]{1,0:T(8,128)(2,1)S(1)}, u32[]{:S(2)}, u32[]{:S(2)}) %collective-permute-start.8) | collective-permute-done | bytes 262176 | tf_op jit(solution)/shard_map/reduce_down/ppermute | solution.py:57
  65.8 3.2 %collective-permute-start.10 = (bf16[96,512]{1,0:T(8,128)(2,1)S(1)}, bf16[96,512]{1,0:T(8,128)(2,1)S(1)}, u32[]{:S(2)}, u32[]{:S(2)}) collective-permute-start(bf16[96,512]{1,0:T(8,128)(2,1)S(1)} %convolution_convert_fusion.2), channel_id=1, source_target_pairs={{0,64},{1,65},{2,66},{3,67},{4,68},{5,69},{6,70},{7,71},{8,72},{9,... | collective-permute-start | bytes 294920 | tf_op jit(solution)/shard_map/back/ppermute | solution.py:57
  69.6 2.6 %collective-permute-start.9 = (bf16[96,512]{1,0:T(8,128)(2,1)S(1)}, bf16[96,512]{1,0:T(8,128)(2,1)S(1)}, u32[]{:S(2)}, u32[]{:S(2)}) collective-permute-start(bf16[96,512]{1,0:T(8,128)(2,1)S(1)} %convolution_convert_fusion.2), channel_id=1, source_target_pairs={{0,96},{1,97},{2,98},{3,99},{4,100},{5,101},{6,102},{7,103},{8,104... | collective-permute-start | bytes 294920 | tf_op jit(solution)/shard_map/back/ppermute | solution.py:57
  72.6 2.2 %collective-permute-done.11 = bf16[96,512]{1,0:T(8,128)(2,1)S(1)} collective-permute-done((bf16[96,512]{1,0:T(8,128)(2,1)S(1)}, bf16[96,512]{1,0:T(8,128)(2,1)S(1)}, u32[]{:S(2)}, u32[]{:S(2)}) %collective-permute-start.11) | collective-permute-done | bytes 98336 | tf_op jit(solution)/shard_map/back/ppermute | solution.py:57
  78.5 6.5 %fusion.105 = f32[1920,1024]{1,0:T(8,128)S(1)} fusion(bf16[1920,1024]{1,0:T(8,128)(2,1)} %all-gather.2.cloned.1.call-done, bf16[1024,1024]{1,0:T(8,128)(2,1)S(1)} %bitcast.118), kind=kOutput, calls=%fused_computation.185 | convolution fusion | flops 4026531840 | bytes 13893632 | tf_op jit(solution)/shard_map/early/dot_general | solution.py:260
  88.0 3.7 %collective-permute-start.15 = (bf16[2,96,1024]{2,1,0:T(8,128)(2,1)S(1)}, bf16[2,96,1024]{2,1,0:T(8,128)(2,1)S(1)}, u32[]{:S(2)}, u32[]{:S(2)}) collective-permute-start(bf16[2,96,1024]{2,1,0:T(8,128)(2,1)S(1)} %bitcast.134), channel_id=1, source_target_pairs={{0,4},{1,5},{2,6},{3,7},{4,8},{5,9},{6,10},{7,11},{8,12},{9,13},{1... | collective-permute-start | bytes 1179656 | tf_op jit(solution)/shard_map/reduce_draft/ppermute | solution.py:57
  93.3 6.2 %collective-permute-start.17 = (bf16[2,96,1024]{2,1,0:T(8,128)(2,1)S(1)}, bf16[2,96,1024]{2,1,0:T(8,128)(2,1)S(1)}, u32[]{:S(2)}, u32[]{:S(2)}) collective-permute-start(bf16[2,96,1024]{2,1,0:T(8,128)(2,1)S(1)} %bitcast.132), channel_id=1, source_target_pairs={{0,12},{1,13},{2,14},{3,15},{4,0},{5,1},{6,2},{7,3},{8,4},{9,5},{1... | collective-permute-start | bytes 1179656 | tf_op jit(solution)/shard_map/reduce_draft/ppermute | solution.py:57
  99.5 2.0 %collective-permute-start.18 = (bf16[2,96,1024]{2,1,0:T(8,128)(2,1)S(1)}, bf16[2,96,1024]{2,1,0:T(8,128)(2,1)S(1)}, u32[]{:S(2)}, u32[]{:S(2)}) collective-permute-start(bf16[2,96,1024]{2,1,0:T(8,128)(2,1)S(1)} %bitcast.133), channel_id=1, source_target_pairs={{0,12},{1,13},{2,14},{3,15},{4,0},{5,1},{6,2},{7,3},{8,4},{9,5},{1... | collective-permute-start | bytes 1179656 | tf_op jit(solution)/shard_map/reduce_draft/ppermute | solution.py:57
  103.8 5.2 %collective-permute-done.18 = bf16[2,96,1024]{2,1,0:T(8,128)(2,1)S(1)} collective-permute-done((bf16[2,96,1024]{2,1,0:T(8,128)(2,1)S(1)}, bf16[2,96,1024]{2,1,0:T(8,128)(2,1)S(1)}, u32[]{:S(2)}, u32[]{:S(2)}) %collective-permute-start.18) | collective-permute-done | bytes 393248 | tf_op jit(solution)/shard_map/reduce_draft/ppermute | solution.py:57
  109.1 3.8 %collective-permute-start.19 = (bf16[2,96,1024]{2,1,0:T(8,128)(2,1)S(1)}, bf16[2,96,1024]{2,1,0:T(8,128)(2,1)S(1)}, u32[]{:S(2)}, u32[]{:S(2)}) collective-permute-start(bf16[2,96,1024]{2,1,0:T(8,128)(2,1)S(1)} %add_convert_fusion.2), channel_id=1, source_target_pairs={{0,12},{1,13},{2,14},{3,15},{4,0},{5,1},{6,2},{7,3},{8,4},{9,5},{1... | collective-permute-start | bytes 1179656 | tf_op jit(solution)/shard_map/reduce_draft/ppermute | solution.py:57
  114.9 3.3 %collective-permute-done.19 = bf16[2,96,1024]{2,1,0:T(8,128)(2,1)S(1)} collective-permute-done((bf16[2,96,1024]{2,1,0:T(8,128)(2,1)S(1)}, bf16[2,96,1024]{2,1,0:T(8,128)(2,1)S(1)}, u32[]{:S(2)}, u32[]{:S(2)}) %collective-permute-start.19) | collective-permute-done | bytes 393248 | tf_op jit(solution)/shard_map/reduce_draft/ppermute | solution.py:57
  119.4 2.4 %collective-permute-start.22 = (bf16[96,1024]{1,0:T(8,128)(2,1)S(1)}, bf16[96,1024]{1,0:T(8,128)(2,1)S(1)}, u32[]{:S(2)}, u32[]{:S(2)}) collective-permute-start(bf16[96,1024]{1,0:T(8,128)(2,1)S(1)} %get-tuple-element.93), channel_id=1, source_target_pairs={{0,3},{1,0},{2,1},{3,2},{4,7},{5,4},{6,5},{7,6},{8,11},{9,8},{10,9... | collective-permute-start | bytes 589832 | tf_op jit(solution)/shard_map/reduce_draft/ppermute | solution.py:57
  122.7 2.7 %collective-permute-done.21 = bf16[96,1024]{1,0:T(8,128)(2,1)S(1)} collective-permute-done((bf16[96,1024]{1,0:T(8,128)(2,1)S(1)}, bf16[96,1024]{1,0:T(8,128)(2,1)S(1)}, u32[]{:S(2)}, u32[]{:S(2)}) %collective-permute-start.21) | collective-permute-done | bytes 196640 | tf_op jit(solution)/shard_map/reduce_draft/ppermute | solution.py:57
  131.0 5.6 %collective-permute-start.26 = (f32[3,96]{1,0:T(4,128)S(1)}, f32[3,96]{1,0:T(4,128)S(1)}, u32[]{:S(2)}, u32[]{:S(2)}) collective-permute-start(f32[3,96]{1,0:T(4,128)S(1)} %fusion.101), channel_id=1, source_target_pairs={{0,64},{1,65},{2,66},{3,67},{4,68},{5,69},{6,70},{7,71},{8,72},{9,... | collective-permute-start | bytes 3464 | tf_op jit(solution)/shard_map/norm/ppermute | solution.py:57
  138.1 2.0 %collective-permute-done.27 = f32[3,96]{1,0:T(4,128)S(1)} collective-permute-done((f32[3,96]{1,0:T(4,128)S(1)}, f32[3,96]{1,0:T(4,128)S(1)}, u32[]{:S(2)}, u32[]{:S(2)}) %collective-permute-start.27) | collective-permute-done | bytes 1184 | tf_op jit(solution)/shard_map/norm/ppermute | solution.py:57
  140.4 7.1 %collective-permute-start.28 = (bf16[96,1024]{1,0:T(8,128)(2,1)S(1)}, bf16[96,1024]{1,0:T(8,128)(2,1)S(1)}, u32[]{:S(2)}, u32[]{:S(2)}) collective-permute-start(bf16[96,1024]{1,0:T(8,128)(2,1)S(1)} %fusion.31), channel_id=1, source_target_pairs={{0,3},{1,0},{2,1},{3,2},{4,7},{5,4},{6,5},{7,6},{8,11},{9,8},{10,9... | collective-permute-start | bytes 589832 | tf_op jit(solution)/shard_map/gather_slope/ppermute | solution.py:57
  148.5 4.2 %collective-permute-done.28 = bf16[96,1024]{1,0:T(8,128)(2,1)S(1)} collective-permute-done((bf16[96,1024]{1,0:T(8,128)(2,1)S(1)}, bf16[96,1024]{1,0:T(8,128)(2,1)S(1)}, u32[]{:S(2)}, u32[]{:S(2)}) %collective-permute-start.28) | collective-permute-done | bytes 196640 | tf_op jit(solution)/shard_map/gather_slope/ppermute | solution.py:57
  152.7 2.0 %collective-permute-done.29 = bf16[96,1024]{1,0:T(8,128)(2,1)S(1)} collective-permute-done((bf16[96,1024]{1,0:T(8,128)(2,1)S(1)}, bf16[96,1024]{1,0:T(8,128)(2,1)S(1)}, u32[]{:S(2)}, u32[]{:S(2)}) %collective-permute-start.29) | collective-permute-done | bytes 196640 | tf_op jit(solution)/shard_map/gather_slope/ppermute | solution.py:57
  156.6 4.9 %collective-permute-start.32 = (bf16[384,1024]{1,0:T(8,128)(2,1)S(1)}, bf16[384,1024]{1,0:T(8,128)(2,1)S(1)}, u32[]{:S(2)}, u32[]{:S(2)}) collective-permute-start(bf16[384,1024]{1,0:T(8,128)(2,1)S(1)} %pad_maximum_fusion.4), channel_id=1, source_target_pairs={{0,12},{1,13},{2,14},{3,15},{4,0},{5,1},{6,2},{7,3},{8,4},{9,5},{1... | collective-permute-start | bytes 2359304 | tf_op jit(solution)/shard_map/gather_slope/ppermute | solution.py:57
  161.5 2.3 %slice.79 = bf16[8,192,1024]{2,1,0:T(8,128)(2,1)S(1)} slice(bf16[8,240,1024]{2,1,0:T(8,128)(2,1)} %bitcast.123), slice={[0:8], [0:192], [0:1024]} | slice | bytes 6291456 | tf_op jit(solution)/shard_map/early/slice | solution.py:267
  165.7 5.8 %collective-permute-done.31 = bf16[384,1024]{1,0:T(8,128)(2,1)S(1)} collective-permute-done((bf16[384,1024]{1,0:T(8,128)(2,1)S(1)}, bf16[384,1024]{1,0:T(8,128)(2,1)S(1)}, u32[]{:S(2)}, u32[]{:S(2)}) %collective-permute-start.31) | collective-permute-done | bytes 786464 | tf_op jit(solution)/shard_map/gather_slope/ppermute | solution.py:57
  175.0 2.0 %collective-permute-start.34 = (bf16[192,1024]{1,0:T(8,128)(2,1)S(1)}, bf16[192,1024]{1,0:T(8,128)(2,1)S(1)}, u32[]{:S(2)}, u32[]{:S(2)}) collective-permute-start(bf16[192,1024]{1,0:T(8,128)(2,1)S(1)} %slice.88), channel_id=1, source_target_pairs={{0,12},{1,13},{2,14},{3,15},{4,0},{5,1},{6,2},{7,3},{8,4},{9,5},{1... | collective-permute-start | bytes 1179656 | tf_op jit(solution)/shard_map/gather_slope/ppermute | solution.py:57
  178.8 3.8 %collective-permute-done.33 = bf16[192,1024]{1,0:T(8,128)(2,1)S(1)} collective-permute-done((bf16[192,1024]{1,0:T(8,128)(2,1)S(1)}, bf16[192,1024]{1,0:T(8,128)(2,1)S(1)}, u32[]{:S(2)}, u32[]{:S(2)}) %collective-permute-start.33) | collective-permute-done | bytes 393248 | tf_op jit(solution)/shard_map/gather_slope/ppermute | solution.py:57
  182.7 4.0 %fusion = bf16[1536,1024]{1,0:T(8,128)(2,1)} fusion(f32[3,512,1024]{2,1,0:T(8,128)S(1)} %bitcast.117, f32[1536,1024]{1,0:T(8,128)S(1)} %convolution_add_fusion, s32[]{:T(128)S(6)} %select_n.402, bf16[1536,1024]{1,0:T(8,128)(2,1)S(1)} %bitcast.103, bf16[1536,512]{1,0:T(8,128)(2,1)S(1)} %bitcast.115, bf16[192,1024]{1,0:T(8,128)(2,1)S(1)} %collective-permute-done.34, ...), kind=kOutput, calls=%fused_computation.5 | convolution fusion | flops 1218183168 | bytes 21233668 | tf_op jit(solution)/shard_map/step/dot_general | solution.py:338
  (149 shorter events, 48.3 us)
Async XLA Ops:
  7.2 71.3 %all-gather.2.cloned.1.call-start = ((), (), s32[]{:S(2)}) async-start(), calls=%async_computation | async-start | bytes 4423680 | tf_op jit(solution)/shard_map/all_gather | solution.py:217
  15.7 14.5 %collective-permute-start.3 = (bf16[2,256,512]{2,1,0:T(8,128)(2,1)S(1)}, bf16[2,256,512]{2,1,0:T(8,128)(2,1)S(1)}, u32[]{:S(2)}, u32[]{:S(2)}) collective-permute-start(bf16[2,256,512]{2,1,0:T(8,128)(2,1)S(1)} %copy-done.11), channel_id=1, source_target_pairs={{0,12},{1,13},{2,14},{3,15},{4,0},{5,1},{6,2},{7,3},{8,4},{9,5},{1... | collective-permute-start | bytes 1572872 | tf_op jit(solution)/shard_map/reduce_down/ppermute | solution.py:57
  19.9 16.8 %collective-permute-start = (bf16[2,256,512]{2,1,0:T(8,128)(2,1)}, bf16[2,256,512]{2,1,0:T(8,128)(2,1)S(1)}, u32[]{:S(2)}, u32[]{:S(2)}) collective-permute-start(bf16[2,256,512]{2,1,0:T(8,128)(2,1)} %get-tuple-element.51), channel_id=1, source_target_pairs={{0,4},{1,5},{2,6},{3,7},{4,8},{5,9},{6,10},{7,11},{8,12},{9,13},{1... | collective-permute-start | bytes 1572872 | tf_op jit(solution)/shard_map/reduce_down/ppermute | solution.py:57
  30.3 19.5 %collective-permute-start.5 = (bf16[2,256,512]{2,1,0:T(8,128)(2,1)}, bf16[2,256,512]{2,1,0:T(8,128)(2,1)S(1)}, u32[]{:S(2)}, u32[]{:S(2)}) collective-permute-start(bf16[2,256,512]{2,1,0:T(8,128)(2,1)} %get-tuple-element.56), channel_id=1, source_target_pairs={{0,4},{1,5},{2,6},{3,7},{4,8},{5,9},{6,10},{7,11},{8,12},{9,13},{1... | collective-permute-start | bytes 1572872 | tf_op jit(solution)/shard_map/reduce_down/ppermute | solution.py:57
  31.5 18.4 %collective-permute-start.4 = (bf16[2,256,512]{2,1,0:T(8,128)(2,1)S(1)}, bf16[2,256,512]{2,1,0:T(8,128)(2,1)S(1)}, u32[]{:S(2)}, u32[]{:S(2)}) collective-permute-start(bf16[2,256,512]{2,1,0:T(8,128)(2,1)S(1)} %add_convert_fusion), channel_id=1, source_target_pairs={{0,12},{1,13},{2,14},{3,15},{4,0},{5,1},{6,2},{7,3},{8,4},{9,5},{1... | collective-permute-start | bytes 1572872 | tf_op jit(solution)/shard_map/reduce_down/ppermute | solution.py:57
  34.7 16.6 %collective-permute-start.2 = (bf16[2,256,512]{2,1,0:T(8,128)(2,1)}, bf16[2,256,512]{2,1,0:T(8,128)(2,1)S(1)}, u32[]{:S(2)}, u32[]{:S(2)}) collective-permute-start(bf16[2,256,512]{2,1,0:T(8,128)(2,1)} %get-tuple-element.52), channel_id=1, source_target_pairs={{0,12},{1,13},{2,14},{3,15},{4,0},{5,1},{6,2},{7,3},{8,4},{9,5},{1... | collective-permute-start | bytes 1572872 | tf_op jit(solution)/shard_map/reduce_down/ppermute | solution.py:57
  38.0 13.4 %collective-permute-start.1 = (bf16[2,256,512]{2,1,0:T(8,128)(2,1)S(1)}, bf16[2,256,512]{2,1,0:T(8,128)(2,1)}, u32[]{:S(2)}, u32[]{:S(2)}) collective-permute-start(bf16[2,256,512]{2,1,0:T(8,128)(2,1)S(1)} %add_convert_fusion.1), channel_id=1, source_target_pairs={{0,4},{1,5},{2,6},{3,7},{4,8},{5,9},{6,10},{7,11},{8,12},{9,13},{1... | collective-permute-start | bytes 1572872 | tf_op jit(solution)/shard_map/reduce_down/ppermute | solution.py:57
  53.5 7.8 %collective-permute-start.6 = (bf16[256,512]{1,0:T(8,128)(2,1)}, bf16[256,512]{1,0:T(8,128)(2,1)S(1)}, u32[]{:S(2)}, u32[]{:S(2)}) collective-permute-start(bf16[256,512]{1,0:T(8,128)(2,1)} %get-tuple-element.84), channel_id=1, source_target_pairs={{0,1},{1,2},{2,3},{3,0},{4,5},{5,6},{6,7},{7,4},{8,9},{9,10},{10,1... | collective-permute-start | bytes 786440 | tf_op jit(solution)/shard_map/reduce_down/ppermute | solution.py:57
  55.1 6.4 %collective-permute-start.7 = (bf16[256,512]{1,0:T(8,128)(2,1)S(1)}, bf16[256,512]{1,0:T(8,128)(2,1)S(1)}, u32[]{:S(2)}, u32[]{:S(2)}) collective-permute-start(bf16[256,512]{1,0:T(8,128)(2,1)S(1)} %get-tuple-element.86), channel_id=1, source_target_pairs={{0,3},{1,0},{2,1},{3,2},{4,7},{5,4},{6,5},{7,6},{8,11},{9,8},{10,9... | collective-permute-start | bytes 786440 | tf_op jit(solution)/shard_map/reduce_down/ppermute | solution.py:57
  56.8 8.5 %collective-permute-start.8 = (bf16[256,512]{1,0:T(8,128)(2,1)S(1)}, bf16[256,512]{1,0:T(8,128)(2,1)S(1)}, u32[]{:S(2)}, u32[]{:S(2)}) collective-permute-start(bf16[256,512]{1,0:T(8,128)(2,1)S(1)} %get-tuple-element.85), channel_id=1, source_target_pairs={{0,2},{1,3},{2,0},{3,1},{4,6},{5,7},{6,4},{7,5},{8,10},{9,11},{10,... | collective-permute-start | bytes 786440 | tf_op jit(solution)/shard_map/reduce_down/ppermute | solution.py:57
  65.8 6.7 %collective-permute-start.10 = (bf16[96,512]{1,0:T(8,128)(2,1)S(1)}, bf16[96,512]{1,0:T(8,128)(2,1)S(1)}, u32[]{:S(2)}, u32[]{:S(2)}) collective-permute-start(bf16[96,512]{1,0:T(8,128)(2,1)S(1)} %convolution_convert_fusion.2), channel_id=1, source_target_pairs={{0,64},{1,65},{2,66},{3,67},{4,68},{5,69},{6,70},{7,71},{8,72},{9,... | collective-permute-start | bytes 294920 | tf_op jit(solution)/shard_map/back/ppermute | solution.py:57
  69.0 5.8 %collective-permute-start.11 = (bf16[96,512]{1,0:T(8,128)(2,1)S(1)}, bf16[96,512]{1,0:T(8,128)(2,1)S(1)}, u32[]{:S(2)}, u32[]{:S(2)}) collective-permute-start(bf16[96,512]{1,0:T(8,128)(2,1)S(1)} %convolution_convert_fusion.2), channel_id=1, source_target_pairs={{0,32},{1,33},{2,34},{3,35},{4,36},{5,37},{6,38},{7,39},{8,40},{9,... | collective-permute-start | bytes 294920 | tf_op jit(solution)/shard_map/back/ppermute | solution.py:57
  75.2 9.8 %collective-permute-start.13 = (bf16[96,512]{1,0:T(8,128)(2,1)S(1)}, bf16[96,512]{1,0:T(8,128)(2,1)S(1)}, u32[]{:S(2)}, u32[]{:S(2)}) collective-permute-start(bf16[96,512]{1,0:T(8,128)(2,1)S(1)} %get-tuple-element.105), channel_id=1, source_target_pairs={{0,0},{1,1},{2,16},{3,20},{4,32},{5,33},{6,48},{7,52},{8,64},{9,65... | collective-permute-start | bytes 294920 | tf_op jit(solution)/shard_map/targets/ppermute | solution.py:57
  75.9 9.1 %collective-permute-start.14 = (bf16[96,512]{1,0:T(8,128)(2,1)S(1)}, bf16[96,512]{1,0:T(8,128)(2,1)S(1)}, u32[]{:S(2)}, u32[]{:S(2)}) collective-permute-start(bf16[96,512]{1,0:T(8,128)(2,1)S(1)} %get-tuple-element.104), channel_id=1, source_target_pairs={{0,1},{1,0},{2,20},{3,16},{4,33},{5,32},{6,52},{7,48},{8,65},{9,64... | collective-permute-start | bytes 294920 | tf_op jit(solution)/shard_map/targets/ppermute | solution.py:57
  88.0 15.6 %collective-permute-start.15 = (bf16[2,96,1024]{2,1,0:T(8,128)(2,1)S(1)}, bf16[2,96,1024]{2,1,0:T(8,128)(2,1)S(1)}, u32[]{:S(2)}, u32[]{:S(2)}) collective-permute-start(bf16[2,96,1024]{2,1,0:T(8,128)(2,1)S(1)} %bitcast.134), channel_id=1, source_target_pairs={{0,4},{1,5},{2,6},{3,7},{4,8},{5,9},{6,10},{7,11},{8,12},{9,13},{1... | collective-permute-start | bytes 1179656 | tf_op jit(solution)/shard_map/reduce_draft/ppermute | solution.py:57
  93.3 20.0 %collective-permute-start.17 = (bf16[2,96,1024]{2,1,0:T(8,128)(2,1)S(1)}, bf16[2,96,1024]{2,1,0:T(8,128)(2,1)S(1)}, u32[]{:S(2)}, u32[]{:S(2)}) collective-permute-start(bf16[2,96,1024]{2,1,0:T(8,128)(2,1)S(1)} %bitcast.132), channel_id=1, source_target_pairs={{0,12},{1,13},{2,14},{3,15},{4,0},{5,1},{6,2},{7,3},{8,4},{9,5},{1... | collective-permute-start | bytes 1179656 | tf_op jit(solution)/shard_map/reduce_draft/ppermute | solution.py:57
  99.5 9.5 %collective-permute-start.18 = (bf16[2,96,1024]{2,1,0:T(8,128)(2,1)S(1)}, bf16[2,96,1024]{2,1,0:T(8,128)(2,1)S(1)}, u32[]{:S(2)}, u32[]{:S(2)}) collective-permute-start(bf16[2,96,1024]{2,1,0:T(8,128)(2,1)S(1)} %bitcast.133), channel_id=1, source_target_pairs={{0,12},{1,13},{2,14},{3,15},{4,0},{5,1},{6,2},{7,3},{8,4},{9,5},{1... | collective-permute-start | bytes 1179656 | tf_op jit(solution)/shard_map/reduce_draft/ppermute | solution.py:57
  101.5 13.4 %collective-permute-start.20 = (bf16[2,96,1024]{2,1,0:T(8,128)(2,1)S(1)}, bf16[2,96,1024]{2,1,0:T(8,128)(2,1)S(1)}, u32[]{:S(2)}, u32[]{:S(2)}) collective-permute-start(bf16[2,96,1024]{2,1,0:T(8,128)(2,1)S(1)} %bitcast.131), channel_id=1, source_target_pairs={{0,4},{1,5},{2,6},{3,7},{4,8},{5,9},{6,10},{7,11},{8,12},{9,13},{1... | collective-permute-start | bytes 1179656 | tf_op jit(solution)/shard_map/reduce_draft/ppermute | solution.py:57
  103.7 11.0 %collective-permute-start.16 = (bf16[2,96,1024]{2,1,0:T(8,128)(2,1)S(1)}, bf16[2,96,1024]{2,1,0:T(8,128)(2,1)S(1)}, u32[]{:S(2)}, u32[]{:S(2)}) collective-permute-start(bf16[2,96,1024]{2,1,0:T(8,128)(2,1)S(1)} %add_convert_fusion.3), channel_id=1, source_target_pairs={{0,4},{1,5},{2,6},{3,7},{4,8},{5,9},{6,10},{7,11},{8,12},{9,13},{1... | collective-permute-start | bytes 1179656 | tf_op jit(solution)/shard_map/reduce_draft/ppermute | solution.py:57
  109.1 9.1 %collective-permute-start.19 = (bf16[2,96,1024]{2,1,0:T(8,128)(2,1)S(1)}, bf16[2,96,1024]{2,1,0:T(8,128)(2,1)S(1)}, u32[]{:S(2)}, u32[]{:S(2)}) collective-permute-start(bf16[2,96,1024]{2,1,0:T(8,128)(2,1)S(1)} %add_convert_fusion.2), channel_id=1, source_target_pairs={{0,12},{1,13},{2,14},{3,15},{4,0},{5,1},{6,2},{7,3},{8,4},{9,5},{1... | collective-permute-start | bytes 1179656 | tf_op jit(solution)/shard_map/reduce_draft/ppermute | solution.py:57
  118.5 6.9 %collective-permute-start.21 = (bf16[96,1024]{1,0:T(8,128)(2,1)S(1)}, bf16[96,1024]{1,0:T(8,128)(2,1)S(1)}, u32[]{:S(2)}, u32[]{:S(2)}) collective-permute-start(bf16[96,1024]{1,0:T(8,128)(2,1)S(1)} %get-tuple-element.91), channel_id=1, source_target_pairs={{0,1},{1,2},{2,3},{3,0},{4,5},{5,6},{6,7},{7,4},{8,9},{9,10},{10,1... | collective-permute-start | bytes 589832 | tf_op jit(solution)/shard_map/reduce_draft/ppermute | solution.py:57
  119.4 7.7 %collective-permute-start.22 = (bf16[96,1024]{1,0:T(8,128)(2,1)S(1)}, bf16[96,1024]{1,0:T(8,128)(2,1)S(1)}, u32[]{:S(2)}, u32[]{:S(2)}) collective-permute-start(bf16[96,1024]{1,0:T(8,128)(2,1)S(1)} %get-tuple-element.93), channel_id=1, source_target_pairs={{0,3},{1,0},{2,1},{3,2},{4,7},{5,4},{6,5},{7,6},{8,11},{9,8},{10,9... | collective-permute-start | bytes 589832 | tf_op jit(solution)/shard_map/reduce_draft/ppermute | solution.py:57
  121.8 7.2 %collective-permute-start.23 = (bf16[96,1024]{1,0:T(8,128)(2,1)S(1)}, bf16[96,1024]{1,0:T(8,128)(2,1)S(1)}, u32[]{:S(2)}, u32[]{:S(2)}) collective-permute-start(bf16[96,1024]{1,0:T(8,128)(2,1)S(1)} %get-tuple-element.92), channel_id=1, source_target_pairs={{0,2},{1,3},{2,0},{3,1},{4,6},{5,7},{6,4},{7,5},{8,10},{9,11},{10,... | collective-permute-start | bytes 589832 | tf_op jit(solution)/shard_map/reduce_draft/ppermute | solution.py:57
  130.6 6.1 %collective-permute-start.25 = (f32[3,96]{1,0:T(4,128)S(1)}, f32[3,96]{1,0:T(4,128)S(1)}, u32[]{:S(2)}, u32[]{:S(2)}) collective-permute-start(f32[3,96]{1,0:T(4,128)S(1)} %fusion.101), channel_id=1, source_target_pairs={{0,32},{1,33},{2,34},{3,35},{4,36},{5,37},{6,38},{7,39},{8,40},{9,... | collective-permute-start | bytes 3464 | tf_op jit(solution)/shard_map/norm/ppermute | solution.py:57
  131.0 7.1 %collective-permute-start.26 = (f32[3,96]{1,0:T(4,128)S(1)}, f32[3,96]{1,0:T(4,128)S(1)}, u32[]{:S(2)}, u32[]{:S(2)}) collective-permute-start(f32[3,96]{1,0:T(4,128)S(1)} %fusion.101), channel_id=1, source_target_pairs={{0,64},{1,65},{2,66},{3,67},{4,68},{5,69},{6,70},{7,71},{8,72},{9,... | collective-permute-start | bytes 3464 | tf_op jit(solution)/shard_map/norm/ppermute | solution.py:57
  140.4 12.4 %collective-permute-start.28 = (bf16[96,1024]{1,0:T(8,128)(2,1)S(1)}, bf16[96,1024]{1,0:T(8,128)(2,1)S(1)}, u32[]{:S(2)}, u32[]{:S(2)}) collective-permute-start(bf16[96,1024]{1,0:T(8,128)(2,1)S(1)} %fusion.31), channel_id=1, source_target_pairs={{0,3},{1,0},{2,1},{3,2},{4,7},{5,4},{6,5},{7,6},{8,11},{9,8},{10,9... | collective-permute-start | bytes 589832 | tf_op jit(solution)/shard_map/gather_slope/ppermute | solution.py:57
  147.4 7.3 %collective-permute-start.29 = (bf16[96,1024]{1,0:T(8,128)(2,1)S(1)}, bf16[96,1024]{1,0:T(8,128)(2,1)S(1)}, u32[]{:S(2)}, u32[]{:S(2)}) collective-permute-start(bf16[96,1024]{1,0:T(8,128)(2,1)S(1)} %fusion.31), channel_id=1, source_target_pairs={{0,2},{1,3},{2,0},{3,1},{4,6},{5,7},{6,4},{7,5},{8,10},{9,11},{10,... | collective-permute-start | bytes 589832 | tf_op jit(solution)/shard_map/gather_slope/ppermute | solution.py:57
  147.4 9.0 %collective-permute-start.30 = (bf16[96,1024]{1,0:T(8,128)(2,1)S(1)}, bf16[96,1024]{1,0:T(8,128)(2,1)S(1)}, u32[]{:S(2)}, u32[]{:S(2)}) collective-permute-start(bf16[96,1024]{1,0:T(8,128)(2,1)S(1)} %fusion.31), channel_id=1, source_target_pairs={{0,1},{1,2},{2,3},{3,0},{4,5},{5,6},{6,7},{7,4},{8,9},{9,10},{10,1... | collective-permute-start | bytes 589832 | tf_op jit(solution)/shard_map/gather_slope/ppermute | solution.py:57
  156.6 14.9 %collective-permute-start.31 = (bf16[384,1024]{1,0:T(8,128)(2,1)S(1)}, bf16[384,1024]{1,0:T(8,128)(2,1)S(1)}, u32[]{:S(2)}, u32[]{:S(2)}) collective-permute-start(bf16[384,1024]{1,0:T(8,128)(2,1)S(1)} %pad_maximum_fusion.4), channel_id=1, source_target_pairs={{0,4},{1,5},{2,6},{3,7},{4,8},{5,9},{6,10},{7,11},{8,12},{9,13},{1... | collective-permute-start | bytes 2359304 | tf_op jit(solution)/shard_map/gather_slope/ppermute | solution.py:57
  156.6 14.8 %collective-permute-start.32 = (bf16[384,1024]{1,0:T(8,128)(2,1)S(1)}, bf16[384,1024]{1,0:T(8,128)(2,1)S(1)}, u32[]{:S(2)}, u32[]{:S(2)}) collective-permute-start(bf16[384,1024]{1,0:T(8,128)(2,1)S(1)} %pad_maximum_fusion.4), channel_id=1, source_target_pairs={{0,12},{1,13},{2,14},{3,15},{4,0},{5,1},{6,2},{7,3},{8,4},{9,5},{1... | collective-permute-start | bytes 2359304 | tf_op jit(solution)/shard_map/gather_slope/ppermute | solution.py:57
  173.5 9.1 %collective-permute-start.33 = (bf16[192,1024]{1,0:T(8,128)(2,1)S(1)}, bf16[192,1024]{1,0:T(8,128)(2,1)S(1)}, u32[]{:S(2)}, u32[]{:S(2)}) collective-permute-start(bf16[192,1024]{1,0:T(8,128)(2,1)S(1)} %slice.87), channel_id=1, source_target_pairs={{0,4},{1,5},{2,6},{3,7},{4,8},{5,9},{6,10},{7,11},{8,12},{9,13},{1... | collective-permute-start | bytes 1179656 | tf_op jit(solution)/shard_map/gather_slope/ppermute | solution.py:57
  175.0 7.8 %collective-permute-start.34 = (bf16[192,1024]{1,0:T(8,128)(2,1)S(1)}, bf16[192,1024]{1,0:T(8,128)(2,1)S(1)}, u32[]{:S(2)}, u32[]{:S(2)}) collective-permute-start(bf16[192,1024]{1,0:T(8,128)(2,1)S(1)} %slice.88), channel_id=1, source_target_pairs={{0,12},{1,13},{2,14},{3,15},{4,0},{5,1},{6,2},{7,3},{8,4},{9,5},{1... | collective-permute-start | bytes 1179656 | tf_op jit(solution)/shard_map/gather_slope/ppermute | solution.py:57
  (23 other events, 133.5 us)
Sparse Core Ops, SparseCore 0:
  15.8 33.4 all-gather.1
